TPU v7x, 256 devices: a whole 4x4x8 slice. The times are simulated.
256 devices in a mesh: blk: 64 (over y_lo, z, x), row: 4 (over y_hi, core).
Axes of the slice: x: 4, y: 4 (y_hi: 2, y_lo: 2; y = y_hi * 2 + y_lo), z: 8, core: 2. Of those that a mesh axis runs over, the one named last changes fastest.
Arguments:
- transmission: float32 [16384, 2, 8192], P(('blk', 'row')), may hold values from -64 to 64, as said below
- assignment: int32 [256], replicated, may hold values from 0 to 255, each once
- pairing: int32 [2, 64], replicated, may hold values from 0 to 2
Outputs:
- rotated: float32 [16384, 2, 8192], P(('blk', 'row'))
Inputs may be any that keep to these rules, and one draw needn't show every extreme that they name: `transmission`: entries are real and imaginary parts of a measured speckle field; columns and rows have differing gains. `assignment`: A permutation of the block numbers.
All inputs are finite; a program needn't handle non-finite values.
Results may differ from a plain program's by a relative error of at most 0.00016.
Values sent between devices are 32-bit elements; how exact they have to be, the bound alone decides.
A program may use at most 128 MiB of HBM per device.

v0:
```python
import jax
import jax.numpy as jnp
from jax import lax
from jax.sharding import PartitionSpec as P

ROWS = 16384
BLOCK = 32
SLOTS = 4
ROUNDS = 2
NS_STEPS = 6


def shifted(block, axis, distance):
    devices = range(lax.axis_size(axis))
    route = [((i - distance) % len(devices), i) for i in devices]
    return lax.ppermute(block, axis, route)


def kernel_rotation(real_part, imag_part):
    kernel = jnp.concatenate(
        [
            jnp.concatenate([real_part, imag_part], axis=1),
            jnp.concatenate([-imag_part, real_part], axis=1),
        ],
        axis=0,
    )
    scale = jnp.sqrt(jnp.sum(kernel * kernel))
    eye = jnp.eye(kernel.shape[0], dtype=jnp.float32)
    upper = kernel / scale
    lower = eye
    for step in range(NS_STEPS):
        middle = 1.5 * eye - 0.5 * jnp.dot(lower, upper, precision=lax.Precision.HIGHEST)
        upper = jnp.dot(upper, middle, precision=lax.Precision.HIGHEST)
        lower = jnp.dot(middle, lower, precision=lax.Precision.HIGHEST)
    return lower * jnp.sqrt(ROWS / scale)


def pair_rotation(gram):
    half = gram.shape[0] // 2
    real_part = gram[:half, :half] + gram[half:, half:]
    imag_part = gram[:half, half:] - gram[half:, :half]
    return kernel_rotation(real_part, imag_part)


def local_gram(joined):
    return jnp.dot(joined.T, joined, precision=lax.Precision.HIGHEST)


def summed_pair(joined):
    gram = lax.psum(local_gram(joined), "row")
    return jnp.dot(joined, pair_rotation(gram), precision=lax.Precision.HIGHEST)


def column_index(held, total_cols):
    parts = jnp.arange(2, dtype=jnp.int32)[None, :, None, None] * total_cols
    starts = held[:, None, :, None] * BLOCK
    within = jnp.arange(BLOCK, dtype=jnp.int32)[None, None, None, :]
    return (parts + starts + within).reshape(-1)


def slot_columns(slots):
    parts = jnp.arange(2, dtype=jnp.int32)[:, None, None] * (SLOTS * BLOCK)
    starts = slots[None, :, None] * BLOCK
    within = jnp.arange(BLOCK, dtype=jnp.int32)[None, None, :]
    return (parts + starts + within).reshape(-1)


def inverse_of(index):
    return (
        jnp.zeros(index.shape, jnp.int32).at[index].set(jnp.arange(index.shape[0], dtype=jnp.int32))
    )


def turn_held(held):
    return jnp.stack(
        [held[:, 0], jnp.roll(held[:, 1], 1), jnp.roll(held[:, 2], -1), held[:, 3]], axis=1
    )


def on_device(transmission, assignment, pairing):
    nblk = lax.axis_size("blk")
    me_blk = lax.axis_index("blk")
    row_part = transmission.shape[0]
    total_cols = transmission.shape[2]
    orders = jnp.array([[0, 1, 2, 3], [0, 2, 1, 3], [0, 3, 1, 2]], dtype=jnp.int32)
    held = assignment.reshape(nblk, SLOTS)
    flat = transmission.reshape(row_part, 2 * total_cols)
    outgoing = jnp.take(flat, column_index(held, total_cols), axis=1)
    blocks = lax.all_to_all(outgoing, "blk", split_axis=1, concat_axis=0, tiled=True)
    owned_rows = blocks.shape[0]
    for rnd in range(ROUNDS):
        pick = pairing[rnd, me_blk]
        order = orders[pick]
        first_cols = slot_columns(order[0:2])
        second_cols = slot_columns(order[2:4])
        first = jnp.take(blocks, first_cols, axis=1)
        second = jnp.take(blocks, second_cols, axis=1)
        new_first = summed_pair(first)
        new_second = summed_pair(second)
        joined = jnp.concatenate([new_first, new_second], axis=1)
        back = inverse_of(jnp.concatenate([first_cols, second_cols]))
        blocks = jnp.take(joined, back, axis=1)
        if rnd < ROUNDS - 1:
            lanes = owned_rows * 2 * BLOCK // 128
            up_cols = slot_columns(jnp.array([1], dtype=jnp.int32))
            down_cols = slot_columns(jnp.array([2], dtype=jnp.int32))
            moved_up = shifted(jnp.take(blocks, up_cols, axis=1).reshape(lanes, 128), "blk", 1)
            moved_down = shifted(jnp.take(blocks, down_cols, axis=1).reshape(lanes, 128), "blk", -1)
            blocks = blocks.at[:, up_cols].set(moved_up.reshape(owned_rows, 2 * BLOCK))
            blocks = blocks.at[:, down_cols].set(moved_down.reshape(owned_rows, 2 * BLOCK))
            held = turn_held(held)
    returned = lax.all_to_all(blocks, "blk", split_axis=0, concat_axis=1, tiled=True)
    placed = column_index(held, total_cols)
    rotated = jnp.take(returned, inverse_of(placed), axis=1)
    return rotated.reshape(row_part, 2, total_cols)


def solution(mesh):
    placed = (P(("blk", "row"), None, None), P(), P())
    return jax.shard_map(
        on_device,
        mesh=mesh,
        in_specs=placed,
        out_specs=P(("blk", "row"), None, None),
        check_vma=False,
    )
```

profile of v0, /device:TPU:1, one launch (start us, length us, event | category | flops | bytes accessed | tf_op | source)
XLA Modules:
  0.0 664.3 jit_solution(6179644993815325899)
XLA Ops:
  8.3 1.4 add_bitcast_fusion
  10.4 8.4 %copy.43 = f32[64,2,8192]{0,2,1:T(8,128)} copy(f32[64,2,8192]{2,1,0:T(2,128)} %param.14) | data formatting | bytes 8388608 | tf_op args[0]
  18.8 58.2 %gather_fusion = f32[16384,64]{1,0:T(8,128)} fusion(f32[64,16384]{0,1:T(8,128)} %bitcast.203, s32[16384]{0:T(1024)S(1)} %fusion.68), kind=kCustom, calls=%fused_computation.clone | custom fusion | bytes 8454144 | tf_op jit(solution)/shard_map/jit(_take)/gather | solution.py:88
  77.0 13.1 %broadcast_select_fusion.1 = f32[16384,64]{1,0:T(8,128)} fusion(f32[16384,64]{1,0:T(8,128)} %gather_fusion, pred[16384]{0:T(1024)(128)(4,1)S(1)} %compare_and_fusion.1), kind=kLoop, calls=%fused_computation.20 | loop fusion | flops 1048576 | bytes 8404992 | tf_op jit(solution)/shard_map/jit(_take)/select_n | solution.py:88
  90.1 6.8 %copy.44 = f32[64,64,256]{2,0,1:T(8,128)} copy(f32[64,64,256]{0,2,1:T(8,128)} %bitcast.204) | data formatting | bytes 8388608 | tf_op jit(solution)/shard_map/all_to_all | solution.py:89
  96.9 13.9 %all-to-all-start = ((f32[64,64,256]{2,0,1:T(8,128)}), f32[64,64,256]{2,0,1:T(8,128)}, u32[]{:S(2)}, u32[]{:S(2)}) async-start(f32[64,64,256]{2,0,1:T(8,128)} %copy.44), calls=%async_computation | async-start | bytes 8388608 | tf_op jit(solution)/shard_map/all_to_all | solution.py:89
  116.7 1.6 scatter_custom_fusion
  118.4 85.1 %all-to-all-done = f32[64,64,256]{2,0,1:T(8,128)} async-done(((f32[64,64,256]{2,0,1:T(8,128)}), f32[64,64,256]{2,0,1:T(8,128)}, u32[]{:S(2)}, u32[]{:S(2)}) %all-to-all-start) | async-done | bytes 4194336 | tf_op jit(solution)/shard_map/all_to_all | solution.py:89
  203.6 5.6 copy.45
  209.2 5.6 gather_fusion.2
  214.8 4.4 gather_fusion.1
  219.2 4.9 fusion.10
  224.1 2.7 fusion.14
  227.3 1.6 scatter_custom_fusion.3
  228.9 43.5 %all-reduce.7.cloned.1.call-done = (f32[128,128]{1,0:T(8,128)}, f32[128,128]{1,0:T(8,128)}) async-done(((f32[128,128]{1,0:T(8,128)}, f32[128,128]{1,0:T(8,128)}), (f32[128,128]{1,0:T(8,128)}, f32[128,128]{1,0:T(8,128)})) %all-reduce.7.cloned.1.call-update) | async-done | bytes 131088 | tf_op jit(solution)/shard_map/psum | solution.py:50
  283.3 5.1 fusion.8
  288.8 2.2 fusion.12
  291.0 2.5 pad_maximum_fusion
  293.5 7.8 %gather_fusion.3 = f32[256,4096]{1,0:T(8,128)} fusion(f32[4096,256]{0,1:T(8,128)} %pad_maximum_fusion, s32[1024]{0:T(1024)S(1)} %pad_clamp_fusion.5), kind=kCustom, calls=%fused_computation.2.clone | custom fusion | bytes 8389632 | tf_op jit(solution)/shard_map/jit(_take)/gather | solution.py:102
  301.3 5.2 select_bitcast_fusion.1
  306.5 3.6 gather_fusion.5
  310.1 3.6 gather_fusion.4
  314.8 1.8 copy.47
  321.2 4.5 collective-permute-start.1
  325.8 21.3 %collective-permute-done = f32[2048,128]{1,0:T(8,128)} collective-permute-done((f32[2048,128]{1,0:T(8,128)}, f32[2048,128]{1,0:T(8,128)}, u32[]{:S(2)}, u32[]{:S(2)}) %collective-permute-start) | collective-permute-done | bytes 1048608 | tf_op jit(solution)/shard_map/ppermute | solution.py:16
  347.1 1.6 reshape.703
  349.3 2.7 reshape.711
  352.0 2.2 copy.50
  354.1 5.3 scatter_fusion
  359.5 5.5 scatter_fusion.1
  365.0 5.6 gather_fusion.7
  370.6 4.4 gather_fusion.6
  375.0 4.9 fusion.2
  379.9 2.7 fusion.6
  382.6 44.7 %all-reduce.5.cloned.1.call-done = (f32[128,128]{1,0:T(8,128)}, f32[128,128]{1,0:T(8,128)}) async-done(((f32[128,128]{1,0:T(8,128)}, f32[128,128]{1,0:T(8,128)}), (f32[128,128]{1,0:T(8,128)}, f32[128,128]{1,0:T(8,128)})) %all-reduce.5.cloned.1.call-update) | async-done | bytes 131088 | tf_op jit(solution)/shard_map/psum | solution.py:50
  438.2 5.3 fusion
  444.0 2.2 fusion.4
  446.2 2.5 pad_maximum_fusion.1
  448.7 7.8 %gather_fusion.8 = f32[256,4096]{1,0:T(8,128)} fusion(f32[4096,256]{0,1:T(8,128)} %pad_maximum_fusion.1, s32[1024]{0:T(1024)S(1)} %pad_clamp_fusion), kind=kCustom, calls=%fused_computation.8.clone | custom fusion | bytes 8389632 | tf_op jit(solution)/shard_map/jit(_take)/gather | solution.py:102
  456.5 4.8 select_bitcast_fusion
  461.3 5.6 copy.51
  466.9 10.4 %all-to-all-start.1 = ((f32[64,64,256]{2,1,0:T(8,128)}), f32[64,64,256]{2,1,0:T(8,128)}, u32[]{:S(2)}, u32[]{:S(2)}) async-start(f32[64,64,256]{2,1,0:T(8,128)} %bitcast.206), calls=%async_computation.1 | async-start | bytes 8388608 | tf_op jit(solution)/shard_map/all_to_all | solution.py:112
  477.9 60.3 %scatter_custom_fusion.4 = s32[16384]{0:T(1024)S(1)} fusion(s32[16384]{0:T(1024)S(1)} %bitcast.209, s32[16384]{0:T(1024)S(1)} %iota.215, s32[]{:T(128)} %constant.15.clone.1), kind=kCustom, calls=%fused_computation.148 | custom fusion | bytes 65540 | tf_op jit(solution)/shard_map/scatter | solution.py:70
  538.3 32.2 %all-to-all-done.1 = f32[64,64,256]{2,1,0:T(8,128)} async-done(((f32[64,64,256]{2,1,0:T(8,128)}), f32[64,64,256]{2,1,0:T(8,128)}, u32[]{:S(2)}, u32[]{:S(2)}) %all-to-all-start.1) | async-done | bytes 4194336 | tf_op jit(solution)/shard_map/all_to_all | solution.py:112
  570.4 6.9 %copy.52 = f32[64,64,256]{0,2,1:T(8,128)} copy(f32[64,64,256]{2,0,1:T(8,128)} %bitcast.32) | data formatting | bytes 8388608 | tf_op jit(solution)/shard_map/all_to_all | solution.py:112
  577.3 58.2 %gather_fusion.9 = f32[16384,64]{1,0:T(8,128)} fusion(f32[64,16384]{0,1:T(8,128)} %bitcast.202, s32[16384]{0:T(1024)S(1)} %fusion.69), kind=kCustom, calls=%fused_computation.4.clone | custom fusion | bytes 8454144 | tf_op jit(solution)/shard_map/jit(_take)/gather | solution.py:114
  635.6 13.1 %broadcast_select_fusion = f32[16384,64]{1,0:T(8,128)} fusion(f32[16384,64]{1,0:T(8,128)} %gather_fusion.9, pred[16384]{0:T(1024)(128)(4,1)S(1)} %compare_and_fusion), kind=kLoop, calls=%fused_computation.19 | loop fusion | flops 1048576 | bytes 8404992 | tf_op jit(solution)/shard_map/jit(_take)/select_n | solution.py:114
  648.6 8.6 %copy.53 = f32[64,2,8192]{2,1,0:T(2,128)} copy(f32[64,2,8192]{0,2,1:T(8,128)} %bitcast.205) | data formatting | bytes 8388608 | tf_op jit(solution)/shard_map/reshape | solution.py:115
  (175 shorter events, 31.0 us)
Async XLA Ops:
  96.9 14.0 %copy-start.4 = (s32[2,64]{1,0:T(2,128)S(1)}, s32[2,64]{1,0:T(2,128)}, u32[]{:S(2)}) copy-start(s32[2,64]{1,0:T(2,128)} %param.16) | copy-start | bytes 1540
  96.9 18.4 %copy-start.5 = (s32[3,4]{1,0:T(4,128)S(1)}, s32[3,4]{1,0:T(4,128)}, u32[]{:S(2)}) copy-start(s32[3,4]{1,0:T(4,128)} %constant.22.clone) | copy-start | bytes 148
  96.9 106.7 %all-to-all-start = ((f32[64,64,256]{2,0,1:T(8,128)}), f32[64,64,256]{2,0,1:T(8,128)}, u32[]{:S(2)}, u32[]{:S(2)}) async-start(f32[64,64,256]{2,0,1:T(8,128)} %copy.44), calls=%async_computation | async-start | bytes 8388608 | tf_op jit(solution)/shard_map/all_to_all | solution.py:89
  110.8 161.6 %all-reduce.7.cloned.1.call-start = ((), (), s32[]{:S(2)}) async-start(), calls=%async_computation.3 | async-start | bytes 262144 | tf_op jit(solution)/shard_map/psum | solution.py:50
  226.8 200.5 %all-reduce.5.cloned.1.call-start = ((), (), s32[]{:S(2)}) async-start(), calls=%async_computation.2 | async-start | bytes 262144 | tf_op jit(solution)/shard_map/psum | solution.py:50
  272.4 5.6 copy-start.2
  288.8 2.2 copy-start
  318.0 29.1 %collective-permute-start = (f32[2048,128]{1,0:T(8,128)}, f32[2048,128]{1,0:T(8,128)}, u32[]{:S(2)}, u32[]{:S(2)}) collective-permute-start(f32[2048,128]{1,0:T(8,128)} %reshape.609), channel_id=1, source_target_pairs={{252,0},{0,4},{4,8},{8,12},{12,16},{16,20},{20,24},{24,28},{28,32}... | collective-permute-start | bytes 3145736 | tf_op jit(solution)/shard_map/ppermute | solution.py:16
  321.2 28.0 %collective-permute-start.1 = (f32[2048,128]{1,0:T(8,128)}, f32[2048,128]{1,0:T(8,128)}, u32[]{:S(2)}, u32[]{:S(2)}) collective-permute-start(f32[2048,128]{1,0:T(8,128)} %reshape.611), channel_id=1, source_target_pairs={{4,0},{8,4},{12,8},{16,12},{20,16},{24,20},{28,24},{32,28},{36,32}... | collective-permute-start | bytes 3145736 | tf_op jit(solution)/shard_map/ppermute | solution.py:16
  427.3 5.6 copy-start.3
  444.0 2.2 copy-start.1
  466.9 103.5 %all-to-all-start.1 = ((f32[64,64,256]{2,1,0:T(8,128)}), f32[64,64,256]{2,1,0:T(8,128)}, u32[]{:S(2)}, u32[]{:S(2)}) async-start(f32[64,64,256]{2,1,0:T(8,128)} %bitcast.206), calls=%async_computation.1 | async-start | bytes 8388608 | tf_op jit(solution)/shard_map/all_to_all | solution.py:112
Sparse Core Ops, SparseCore 0:
  226.9 45.4 all-reduce.6
  382.7 44.5 all-reduce.4
where the time goes:
time: 673 us; the launch traced here: 664 us
  local copies, waits for them, and re-layouts  292 us (43%)
  waiting for transfers between devices  227 us (34%)
  other arithmetic  49.8 us (7%)
  matrix products  44.1 us (7%)
  starting transfers between devices  30.1 us (4%)
  between operations  21.6 us (3%)
    psum x2, waiting for transfers between devices, summed_pair(): gram = lax.psum(local_gram(joined), 'row')  88.2 us
    all_to_all x1, waiting for transfers between devices, on_device(): lax.all_to_all(outgoing, 'blk', split_axis=1, concat_axis=0, tiled=True)  85.1 us
    scatter x3, local copies, waits for them, and re-layouts, inverse_of(): jnp.zeros(index.shape, jnp.int32).at[index]  63.5 us
    gather x1, local copies, waits for them, and re-layouts, on_device(): outgoing = jnp.take(flat, column_index(held, total_cols), axis=1)  58.2 us
    gather x1, local copies, waits for them, and re-layouts, on_device(): rotated = jnp.take(returned, inverse_of(placed), axis=1)  58.2 us
    all_to_all x1, waiting for transfers between devices, on_device(): lax.all_to_all(blocks, 'blk', split_axis=0, concat_axis=1, tiled=True)  32.2 us
    ppermute x2, waiting for transfers between devices, shifted(): return lax.ppermute(block, axis, route)  21.3 us
    gather x2, local copies, waits for them, and re-layouts, on_device(): blocks = jnp.take(joined, back, axis=1)  15.6 us
  transfers between devices with their start and end apart: 6, of which 5 were waited for; matrix products, arithmetic and copies ran while one was open for 11% of the time, Pallas kernels for 0%

commit v1 on v0

v1 whole, which is shorter than its diff:
```python
import functools

import jax
import jax.numpy as jnp
from jax import lax
from jax.experimental import pallas as pl
from jax.experimental.pallas import tpu as pltpu
from jax.sharding import PartitionSpec as P

ROWS = 16384
BLOCK = 32
SLOTS = 4
NS_STEPS = 6
UNITS = 64
BLOCKS = 256
MESH = pl.DeviceIdType.MESH
F32 = jnp.float32
BF16 = jnp.bfloat16
NX, NY, NZ = 4, 4, 8
NXY = NX * NY
CHUNK = UNITS // 2 // NXY
SLICE = 64 // NZ
PARAMS = functools.partial(pltpu.CompilerParams, vmem_limit_bytes=56 * 1024 * 1024)


def pair_blocks(assign, pairing, rnd, d, h):
    pick = pairing[rnd, d]
    if h == 0:
        slots = (0, 1 + pick)
    else:
        slots = (jnp.where(pick == 0, 2, 1), jnp.where(pick == 2, 2, 3))

    def block(slot):
        index = d
        if rnd == 1:
            turn = jnp.where(slot == 1, -1, jnp.where(slot == 2, 1, 0))
            index = lax.rem(d + turn + UNITS, UNITS)
        return assign[index * SLOTS + slot]

    return block(slots[0]), block(slots[1])


def lanes_of(shape):
    return lax.broadcasted_iota(jnp.int32, shape, 1)


def rows_of(shape):
    return lax.broadcasted_iota(jnp.int32, shape, 0)


def split(value):
    high = value.astype(BF16)
    return high, (value - high.astype(F32)).astype(BF16)


def turned(pair):
    rolled = pltpu.roll(pair, 64, 1)
    return jnp.where(lanes_of(pair.shape) < 64, rolled, -rolled)


def unpack(unit):
    lane, row = lanes_of(unit.shape), rows_of(unit.shape)
    left = lane < 64
    column = jnp.where(left, lane, lane - 64)
    flipped = jnp.concatenate([unit, unit], axis=0).T
    rolled = pltpu.roll(unit, 64, 1)
    tops = []
    for h in range(2):
        here = jnp.where(left, unit, rolled) if h == 0 else jnp.where(left, rolled, unit)
        there = flipped[64 * h : 64 * h + 64]
        real = jnp.where(row <= column, here, there)
        imag = jnp.where(row > column, here, jnp.where(row < column, -there, 0.0))
        tops.append(jnp.where(left, real, imag))
    return tops


def pack(first, second):
    lane, row = lanes_of(first.shape), rows_of(first.shape)
    left = lane < 64
    packed_first = jnp.where(row <= lane, first, pltpu.roll(first, 64, 1))
    packed_second = jnp.where(row <= lane - 64, pltpu.roll(second, 64, 1), second)
    return jnp.where(left, packed_first, packed_second)


def both(pair):
    return jnp.concatenate([pair, turned(pair)], axis=0)


def nt_dot(a, b):
    return lax.dot_general(a, b, (((1,), (1,)), ((), ())), preferred_element_type=F32)


def gram_top(pair):
    high, low = split(both(pair))
    lhs = jnp.concatenate([high[:64], low[:64]], axis=1)
    rhs = jnp.concatenate([high, high], axis=1)
    return nt_dot(lhs, rhs) + nt_dot(high[:64], low)


def applied(top, pair):
    high, low = split(both(pair))
    whigh, wlow = split(top)
    lhs = jnp.concatenate([whigh, wlow], axis=1)
    rhs = jnp.concatenate([high, high], axis=0)
    return jnp.dot(lhs, rhs, preferred_element_type=F32) + jnp.dot(
        whigh, low, preferred_element_type=F32
    )


def load_pair(table, a, b):
    return jnp.concatenate([table[a], table[b]], axis=0)


def grams(assign, pairing, rnd, table, packed):
    def unit(d, carry):
        tops = []
        for h in range(2):
            a, b = pair_blocks(assign, pairing, rnd, d, h)
            tops.append(gram_top(load_pair(table, a, b)))
        packed[d] = pack(*tops)
        return carry

    lax.fori_loop(0, UNITS, unit, 0, unroll=2)


def apply_all(assign, pairing, rnd, weights, source, target):
    def unit(d, carry):
        tops = unpack(weights[d])
        for h in range(2):
            a, b = pair_blocks(assign, pairing, rnd, d, h)
            new = applied(tops[h], load_pair(source, a, b))
            target[a] = new[:BLOCK]
            target[b] = new[BLOCK:]
        return carry

    lax.fori_loop(0, UNITS, unit, 0, unroll=2)


def first_kernel(assign, pairing, x, table, packed):
    def tile(ct, carry):
        real = x[pl.ds(2 * ct, 64, stride=128), :]
        imag = x[pl.ds(2 * ct + 1, 64, stride=128), :]
        flipped = jnp.concatenate([real, imag], axis=0).T
        table[pl.ds(4 * ct, 4)] = flipped.reshape(4, BLOCK, 128)
        return carry

    lax.fori_loop(0, 64, tile, 0, unroll=2)
    grams(assign, pairing, 0, table, packed)


def middle_kernel(assign, pairing, weights, source, table, packed):
    apply_all(assign, pairing, 0, weights, source, table)
    grams(assign, pairing, 1, table, packed)


def last_kernel(assign, pairing, weights, source, out, table):
    apply_all(assign, pairing, 1, weights, source, table)

    def tile(ct, carry):
        flipped = table[pl.ds(4 * ct, 4)].reshape(128, 128).T
        out[pl.ds(2 * ct, 64, stride=128), :] = flipped[:64]
        out[pl.ds(2 * ct + 1, 64, stride=128), :] = flipped[64:]
        return carry

    lax.fori_loop(0, 64, tile, 0, unroll=2)


def full(top):
    rolled = pltpu.roll(top, 64, 1)
    return jnp.concatenate([top, jnp.where(lanes_of(top.shape) < 64, -rolled, rolled)], axis=0)


def split3(value):
    first, second = split(value)
    rest = value - first.astype(F32) - second.astype(F32)
    return first, second, rest.astype(BF16)


def fdot(a, b):
    a1, a2, a3 = split3(a)
    b1, b2, b3 = split3(b)
    wide = jnp.concatenate([b1, b2], axis=1)
    main = jnp.dot(
        jnp.concatenate([a1, a2], axis=1),
        jnp.concatenate([wide, wide], axis=0),
        preferred_element_type=F32,
    )
    rest = jnp.dot(
        jnp.concatenate([a1, a3], axis=1),
        jnp.concatenate([b3, b1], axis=0),
        preferred_element_type=F32,
    )
    return main[:, :128] + (main[:, 128:] + rest)


def inverse_roots(tops):
    shape = tops[0].shape
    eye = jnp.where(lanes_of(shape) == rows_of(shape), 1.0, 0.0).astype(F32)
    scales = [jnp.sqrt(2.0 * jnp.sum(t * t, axis=(0, 1), keepdims=True)) for t in tops]
    upper = [t / s for t, s in zip(tops, scales)]
    lower = [1.5 * eye - 0.5 * u for u in upper]
    upper = [fdot(u, full(m)) for u, m in zip(upper, lower)]

    def step(_, carry):
        up, low = carry
        middle = [1.5 * eye - 0.5 * fdot(z, full(y)) for y, z in zip(up, low)]
        return (
            [fdot(y, full(m)) for y, m in zip(up, middle)],
            [fdot(m, full(z)) for z, m in zip(low, middle)],
        )

    upper, lower = lax.fori_loop(0, NS_STEPS - 2, step, (upper, lower))
    middle = [1.5 * eye - 0.5 * fdot(z, full(y)) for y, z in zip(upper, lower)]
    lower = [fdot(m, full(z)) for z, m in zip(lower, middle)]
    return [z * jnp.sqrt(ROWS / s) for z, s in zip(lower, scales)]


def reduce_kernel(
    packed, weights, from_core, from_xy, total, slices, from_z, mine_z, gathered,
    core_send, core_recv, xy_send, xy_recv, zr_send, zr_recv, zg_send, zg_recv,
    wxy_send, wxy_recv, wcore_send, wcore_recv,
):
    blk, row = lax.axis_index("blk"), lax.axis_index("row")
    y_lo, z, x = blk // (NZ * NX), lax.rem(blk // NX, NZ), lax.rem(blk, NX)
    y_hi, core = row // 2, lax.rem(row, 2)
    y = y_hi * 2 + y_lo
    me = y * NX + x
    half = UNITS // 2

    def device(yy, zz, xx, cc):
        return (lax.rem(yy, 2) * (NZ * NX) + zz * NX + xx, (yy // 2) * 2 + cc)

    def plane(step):
        return lax.rem(y + step // NX, NY), lax.rem(x + lax.rem(step, NX), NX)

    def plane_back(step):
        return lax.rem(y - step // NX + NY, NY), lax.rem(x - lax.rem(step, NX) + NX, NX)

    partner = device(y, z, x, 1 - core)

    def plane_device(step):
        yy, xx = plane(step)
        return device(yy, z, xx, core)

    def ring_device(step):
        return device(y, lax.rem(z + step, NZ), x, core)

    barrier = pltpu.get_barrier_semaphore()
    pl.semaphore_signal(barrier, inc=1, device_id=partner, device_id_type=MESH)

    def greet_plane(step, carry):
        pl.semaphore_signal(barrier, inc=1, device_id=plane_device(step), device_id_type=MESH)
        return carry

    def greet_ring(step, carry):
        pl.semaphore_signal(barrier, inc=1, device_id=ring_device(step), device_id_type=MESH)
        return carry

    lax.fori_loop(1, NXY, greet_plane, 0)
    lax.fori_loop(1, NZ, greet_ring, 0)
    pl.semaphore_wait(barrier, NXY + NZ - 1)

    def core_copy():
        return pltpu.make_async_remote_copy(
            src_ref=packed.at[pl.ds((1 - core) * half, half)],
            dst_ref=from_core,
            send_sem=core_send,
            recv_sem=core_recv,
            device_id=partner,
            device_id_type=MESH,
        )

    core_copy().start()
    core_copy().wait_recv()

    def xy_copy(step):
        yy, xx = plane(step)
        return pltpu.make_async_remote_copy(
            src_ref=from_core.at[pl.ds((yy * NX + xx) * CHUNK, CHUNK)],
            dst_ref=from_xy.at[step],
            send_sem=xy_send.at[step],
            recv_sem=xy_recv.at[step],
            device_id=device(yy, z, xx, core),
            device_id_type=MESH,
        )

    def chunk_sum(step):
        yy, xx = plane(step)
        place = pl.ds((yy * NX + xx) * CHUNK, CHUNK)
        return from_core[place] + packed[pl.ds(core * half + (yy * NX + xx) * CHUNK, CHUNK)]

    def send_xy(step, carry):
        yy, xx = plane(step)
        from_core[pl.ds((yy * NX + xx) * CHUNK, CHUNK)] = chunk_sum(step)
        xy_copy(step).start()
        return carry

    lax.fori_loop(1, NXY, send_xy, 0)
    total[...] = chunk_sum(0)

    def add_xy(step, carry):
        xy_copy(step).wait_recv()
        total[...] += from_xy[step]
        return carry

    lax.fori_loop(1, NXY, add_xy, 0)

    for k in range(NZ):
        slices[k] = total[:, k * SLICE : (k + 1) * SLICE, :]

    def zr_copy(step):
        return pltpu.make_async_remote_copy(
            src_ref=slices.at[lax.rem(z + step, NZ)],
            dst_ref=from_z.at[step],
            send_sem=zr_send.at[step],
            recv_sem=zr_recv.at[step],
            device_id=ring_device(step),
            device_id_type=MESH,
        )

    def send_zr(step, carry):
        zr_copy(step).start()
        return carry

    def add_zr(step, acc):
        zr_copy(step).wait_recv()
        return acc + from_z[step]

    lax.fori_loop(1, NZ, send_zr, 0)
    mine_z[...] = lax.fori_loop(1, NZ, add_zr, slices[z])
    gathered[z] = mine_z[...]

    def zg_copy(step):
        return pltpu.make_async_remote_copy(
            src_ref=mine_z,
            dst_ref=gathered.at[z],
            send_sem=zg_send.at[step],
            recv_sem=zg_recv.at[step],
            device_id=ring_device(step),
            device_id_type=MESH,
        )

    def send_zg(step, carry):
        zg_copy(step).start()
        return carry

    def recv_zg(step, carry):
        zg_copy(step).wait_recv()
        return carry

    lax.fori_loop(1, NZ, send_zg, 0)
    lax.fori_loop(1, NZ, recv_zg, 0)

    tops = []
    for u in range(CHUNK):
        tops.extend(unpack(gathered[:, u].reshape(64, 128)))
    roots = inverse_roots(tops)
    first = core * half + me * CHUNK
    for u in range(CHUNK):
        weights[first + u] = pack(roots[2 * u], roots[2 * u + 1])

    def wxy_copy(step):
        return pltpu.make_async_remote_copy(
            src_ref=weights.at[pl.ds(first, CHUNK)],
            dst_ref=weights.at[pl.ds(first, CHUNK)],
            send_sem=wxy_send.at[step],
            recv_sem=wxy_recv.at[step],
            device_id=plane_device(step),
            device_id_type=MESH,
        )

    def wcore_copy(step):
        yy, xx = plane_back(step)
        place = pl.ds(core * half + (yy * NX + xx) * CHUNK, CHUNK)
        return pltpu.make_async_remote_copy(
            src_ref=weights.at[place],
            dst_ref=weights.at[place],
            send_sem=wcore_send.at[step],
            recv_sem=wcore_recv.at[step],
            device_id=partner,
            device_id_type=MESH,
        )

    def send_wxy(step, carry):
        wxy_copy(step).start()
        return carry

    lax.fori_loop(1, NXY, send_wxy, 0)
    wcore_copy(0).start()

    def forward(step, carry):
        wxy_copy(step).wait_recv()
        wcore_copy(step).start()
        return carry

    lax.fori_loop(1, NXY, forward, 0)

    def finish(step, carry):
        wcore_copy(step).wait_recv()
        wcore_copy(step).wait_send()
        return carry

    lax.fori_loop(0, NXY, finish, 0)
    core_copy().wait_send()

    def drain_xy(step, carry):
        xy_copy(step).wait_send()
        wxy_copy(step).wait_send()
        return carry

    def drain_z(step, carry):
        zr_copy(step).wait_send()
        zg_copy(step).wait_send()
        return carry

    lax.fori_loop(1, NXY, drain_xy, 0)
    lax.fori_loop(1, NZ, drain_z, 0)


SMEM = pl.BlockSpec(memory_space=pltpu.SMEM)
VMEM = pl.BlockSpec(memory_space=pltpu.VMEM)
PACKED = jax.ShapeDtypeStruct((UNITS, 64, 128), F32)
TABLE = jax.ShapeDtypeStruct((BLOCKS, BLOCK, 128), F32)


def reduced_roots(packed):
    dma = pltpu.SemaphoreType.DMA
    return pl.pallas_call(
        reduce_kernel,
        out_shape=PACKED,
        in_specs=[VMEM],
        out_specs=VMEM,
        scratch_shapes=[
            pltpu.VMEM((UNITS // 2, 64, 128), F32),
            pltpu.VMEM((NXY, CHUNK, 64, 128), F32),
            pltpu.VMEM((CHUNK, 64, 128), F32),
            pltpu.VMEM((NZ, CHUNK, SLICE, 128), F32),
            pltpu.VMEM((NZ, CHUNK, SLICE, 128), F32),
            pltpu.VMEM((CHUNK, SLICE, 128), F32),
            pltpu.VMEM((NZ, CHUNK, SLICE, 128), F32),
            dma, dma,
            dma((NXY,)), dma((NXY,)), dma((NZ,)), dma((NZ,)), dma((NZ,)), dma((NZ,)),
            dma((NXY,)), dma((NXY,)), dma((NXY,)), dma((NXY,)),
        ],
        compiler_params=PARAMS(collective_id=0, has_side_effects=True),
        name="reduce_roots",
    )(packed)


def on_device(transmission, assignment, pairing):
    rows, _, cols = transmission.shape
    x = transmission.reshape(rows, 2, cols // 128, 128).transpose(0, 2, 1, 3).reshape(-1, 128)
    table, packed = pl.pallas_call(
        first_kernel,
        out_shape=(TABLE, PACKED),
        in_specs=[SMEM, SMEM, VMEM],
        out_specs=(VMEM, VMEM),
        compiler_params=PARAMS(),
        name="first_grams",
    )(assignment, pairing, x)
    weights = reduced_roots(packed)
    table, packed = pl.pallas_call(
        middle_kernel,
        out_shape=(TABLE, PACKED),
        in_specs=[SMEM, SMEM, VMEM, VMEM],
        out_specs=(VMEM, VMEM),
        compiler_params=PARAMS(),
        name="apply_grams",
    )(assignment, pairing, weights, table)
    weights = reduced_roots(packed)
    out = pl.pallas_call(
        last_kernel,
        out_shape=jax.ShapeDtypeStruct(x.shape, F32),
        in_specs=[SMEM, SMEM, VMEM, VMEM],
        out_specs=VMEM,
        scratch_shapes=[pltpu.VMEM((BLOCKS, BLOCK, 128), F32)],
        compiler_params=PARAMS(),
        name="apply_last",
    )(assignment, pairing, weights, table)
    out = out.reshape(rows, cols // 128, 2, 128).transpose(0, 2, 1, 3)
    return out.reshape(rows, 2, cols)


def solution(mesh):
    placed = (P(("blk", "row"), None, None), P(), P())
    return jax.shard_map(
        on_device,
        mesh=mesh,
        in_specs=placed,
        out_specs=P(("blk", "row"), None, None),
        check_vma=False,
    )
```

time: 673 us -> 192 us (0.29); the launches traced: 664 us -> 191 us
  local copies, waits for them, and re-layouts: 292 us -> 0 us
  waiting for transfers between devices: 227 us -> 0 us
  Pallas kernels: 0 us -> 191 us
  other arithmetic: 49.8 us -> 0 us
  matrix products: 44.1 us -> 0 us
  starting transfers between devices: 30.1 us -> 0 us
  between operations: 21.6 us -> 0.02 us
    pallas_call x0 -> x5, Pallas kernels: none -> 191 us  [the longest x2 118 us: reduced_roots(): pl.pallas_call(reduce_kernel, out_shape=PACKED, in_specs=[VMEM], out_spec...]
    gather x10 -> x0, local copies, waits for them, and re-layouts: 159 us -> none  [the longest x1 58.2 us: on_device(): outgoing = jnp.take(flat, column_index(held, total_cols), axis=1)]
    all_to_all x2 -> x0, waiting for transfers between devices: 117 us -> none  [the longest x1 85.1 us: on_device(): lax.all_to_all(outgoing, 'blk', split_axis=1, concat_axis=0, tiled=True)]
    psum x2 -> x0, waiting for transfers between devices: 88.2 us -> none  [summed_pair(): gram = lax.psum(local_gram(joined), 'row')]
    scatter x5 -> x0, local copies, waits for them, and re-layouts: 74.3 us -> none  [the longest x3 63.5 us: inverse_of(): jnp.zeros(index.shape, jnp.int32).at[index]]
    dot_general x76 -> x0, matrix products: 44.1 us -> none  [the longest x4 15.1 us: local_gram(): return jnp.dot(joined.T, joined, precision=lax.Precision.HIGHEST)]
    select_n x13 -> x0, other arithmetic: 37.5 us -> none  [the longest x1 13.1 us: on_device(): outgoing = jnp.take(flat, column_index(held, total_cols), axis=1)]
    all_to_all x2 -> x0, starting transfers between devices: 24.3 us -> none  [the longest x1 13.9 us: on_device(): lax.all_to_all(outgoing, 'blk', split_axis=1, concat_axis=0, tiled=True)]
  transfers between devices with their start and end apart: 6 -> 0, of which waited for: 5 -> 0; matrix products, arithmetic and copies ran while one was open for 11% -> 0% of each run, Pallas kernels for 0% -> 0%
where the time goes in v1:
time: 192 us; the launch traced here: 191 us
  Pallas kernels  191 us (99%)
    pallas_call x2, Pallas kernels, reduced_roots(): pl.pallas_call(reduce_kernel, out_shape=PACKED, in_specs=[VMEM], out_spec...  118 us
    pallas_call x1, Pallas kernels, on_device(): pl.pallas_call(middle_kernel, out_shape=(TABLE, PACKED), in_specs=[SMEM,...  29.7 us
    pallas_call x1, Pallas kernels, on_device(): pl.pallas_call(first_kernel, out_shape=(TABLE, PACKED), in_specs=[SMEM, S...  22.8 us
    pallas_call x1, Pallas kernels, on_device(): pl.pallas_call(last_kernel, out_shape=jax.ShapeDtypeStruct(x.shape, F32),...  20.5 us

profile of v1, /device:TPU:1, one launch (start us, length us, event | category | flops | bytes accessed | tf_op | source)
XLA Modules:
  0.0 191.4 jit_solution(13417152742110356814)
XLA Ops:
  0.0 22.8 %first_grams.1 = (f32[256,32,128]{2,1,0:T(8,128)}, f32[64,64,128]{2,1,0:T(8,128)}) custom-call(s32[256]{0:T(256)} %assign.5, s32[2,64]{1,0:T(2,128)} %pairing.5, f32[8192,128]{1,0:T(8,128)} %bitcast.10), custom_call_target="tpu_custom_call" | custom-call | tf_op jit(solution)/shard_map/first_grams/pallas_call | solution.py:453
  22.8 62.2 %reduce_roots.2.weights = f32[64,64,128]{2,1,0:T(8,128)} custom-call(f32[64,64,128]{2,1,0:T(8,128)} %get-tuple-element.9.packed), custom_call_target="tpu_custom_call" | custom-call | tf_op jit(solution)/shard_map/reduce_roots/pallas_call | solution.py:428
  85.1 29.7 %apply_grams.1 = (f32[256,32,128]{2,1,0:T(8,128)}, f32[64,64,128]{2,1,0:T(8,128)}) custom-call(s32[256]{0:T(256)} %assign.5, s32[2,64]{1,0:T(2,128)} %pairing.5, f32[64,64,128]{2,1,0:T(8,128)} %reduce_roots.2.weights, f32[256,32,128]{2,1,0:T(8,128)} %get-tuple-element.10.source), custom_call_target="tpu_custom_call" | custom-call | tf_op jit(solution)/shard_map/apply_grams/pallas_call | solution.py:462
  114.8 56.1 %reduce_roots.3.weights = f32[64,64,128]{2,1,0:T(8,128)} custom-call(f32[64,64,128]{2,1,0:T(8,128)} %get-tuple-element.11.packed), custom_call_target="tpu_custom_call" | custom-call | tf_op jit(solution)/shard_map/reduce_roots/pallas_call | solution.py:428
  170.9 20.5 %apply_last.1 = f32[8192,128]{1,0:T(8,128)} custom-call(s32[256]{0:T(256)} %assign.5, s32[2,64]{1,0:T(2,128)} %pairing.5, f32[64,64,128]{2,1,0:T(8,128)} %reduce_roots.3.weights, f32[256,32,128]{2,1,0:T(8,128)} %get-tuple-element.12.source), custom_call_target="tpu_custom_call" | custom-call | tf_op jit(solution)/shard_map/apply_last/pallas_call | solution.py:471

commit v2 on v0

v2 whole, which is shorter than its diff:
```python
import functools

import jax
import jax.numpy as jnp
from jax import lax
from jax.experimental import pallas as pl
from jax.experimental.pallas import tpu as pltpu
from jax.sharding import PartitionSpec as P

ROWS = 16384
BLOCK = 32
SLOTS = 4
NS_STEPS = 6
UNITS = 64
BLOCKS = 256
MESH = pl.DeviceIdType.MESH
F32 = jnp.float32
BF16 = jnp.bfloat16
NX, NY, NZ = 4, 4, 8
NXY = NX * NY
CHUNK = UNITS // 2 // NXY
SLICE = 64 // NZ
PARAMS = functools.partial(pltpu.CompilerParams, vmem_limit_bytes=56 * 1024 * 1024)


def position(pick, slot):
    if_two = jnp.where(slot == 0, 0, jnp.where(slot == 3, 1, slot + 1))
    if_one = jnp.where(slot == 1, 2, jnp.where(slot == 2, 1, slot))
    return jnp.where(pick == 0, slot, jnp.where(pick == 1, if_one, if_two))


def slot_at(pick, h):
    if h == 0:
        return 0, 1 + pick
    return jnp.where(pick == 0, 2, 1), jnp.where(pick == 2, 2, 3)


def turn_of(slot):
    return jnp.where(slot == 1, -1, jnp.where(slot == 2, 1, 0))


def pair_places(assign, pairing, rnd, d, h):
    slots = slot_at(pairing[rnd, d], h)
    if rnd == 0:
        return [assign[d * SLOTS + slot] for slot in slots]
    places = []
    for slot in slots:
        home = lax.rem(d + turn_of(slot) + UNITS, UNITS)
        places.append(home * SLOTS + position(pairing[0, home], slot))
    return places


def lanes_of(shape):
    return lax.broadcasted_iota(jnp.int32, shape, 1)


def rows_of(shape):
    return lax.broadcasted_iota(jnp.int32, shape, 0)


def split(value):
    high = value.astype(BF16)
    return high, (value - high.astype(F32)).astype(BF16)


def turned(pair):
    rolled = pltpu.roll(pair, 64, 1)
    return jnp.where(lanes_of(pair.shape) < 64, rolled, -rolled)


def unpack(unit):
    lane, row = lanes_of(unit.shape), rows_of(unit.shape)
    left = lane < 64
    column = jnp.where(left, lane, lane - 64)
    flipped = jnp.concatenate([unit, unit], axis=0).T
    rolled = pltpu.roll(unit, 64, 1)
    tops = []
    for h in range(2):
        here = jnp.where(left, unit, rolled) if h == 0 else jnp.where(left, rolled, unit)
        there = flipped[64 * h : 64 * h + 64]
        real = jnp.where(row <= column, here, there)
        imag = jnp.where(row > column, here, jnp.where(row < column, -there, 0.0))
        tops.append(jnp.where(left, real, imag))
    return tops


def pack(first, second):
    lane, row = lanes_of(first.shape), rows_of(first.shape)
    left = lane < 64
    packed_first = jnp.where(row <= lane, first, pltpu.roll(first, 64, 1))
    packed_second = jnp.where(row <= lane - 64, pltpu.roll(second, 64, 1), second)
    return jnp.where(left, packed_first, packed_second)


def both(pair):
    return jnp.concatenate([pair, turned(pair)], axis=0)


def nt_dot(a, b):
    return lax.dot_general(a, b, (((1,), (1,)), ((), ())), preferred_element_type=F32)


def gram_top(pair):
    high, low = split(both(pair))
    lhs = jnp.concatenate([high[:64], low[:64]], axis=1)
    rhs = jnp.concatenate([high, high], axis=1)
    return nt_dot(lhs, rhs) + nt_dot(high[:64], low)


def applied(top, pair):
    high, low = split(both(pair))
    whigh, wlow = split(top)
    lhs = jnp.concatenate([whigh, wlow], axis=1)
    rhs = jnp.concatenate([high, high], axis=0)
    return jnp.dot(lhs, rhs, preferred_element_type=F32) + jnp.dot(
        whigh, low, preferred_element_type=F32
    )


def load_pair(table, a, b):
    return jnp.concatenate([table[a], table[b]], axis=0)


def full(top):
    rolled = pltpu.roll(top, 64, 1)
    return jnp.concatenate([top, jnp.where(lanes_of(top.shape) < 64, -rolled, rolled)], axis=0)


def split3(value):
    first, second = split(value)
    rest = value - first.astype(F32) - second.astype(F32)
    return first, second, rest.astype(BF16)


def fdot(a, b):
    a1, a2, a3 = split3(a)
    b1, b2, b3 = split3(b)
    wide = jnp.concatenate([b1, b2], axis=1)
    main = jnp.dot(
        jnp.concatenate([a1, a2], axis=1),
        jnp.concatenate([wide, wide], axis=0),
        preferred_element_type=F32,
    )
    rest = jnp.dot(
        jnp.concatenate([a1, a3], axis=1),
        jnp.concatenate([b3, b1], axis=0),
        preferred_element_type=F32,
    )
    return main[:, :128] + (main[:, 128:] + rest)


def inverse_roots(tops):
    shape = tops[0].shape
    eye = jnp.where(lanes_of(shape) == rows_of(shape), 1.0, 0.0).astype(F32)
    scales = [jnp.sqrt(2.0 * jnp.sum(t * t, axis=(0, 1), keepdims=True)) for t in tops]
    upper = [t / s for t, s in zip(tops, scales)]
    lower = [1.5 * eye - 0.5 * u for u in upper]
    upper = [fdot(u, full(m)) for u, m in zip(upper, lower)]

    def step(_, carry):
        up, low = carry
        middle = [1.5 * eye - 0.5 * fdot(z, full(y)) for y, z in zip(up, low)]
        return (
            [fdot(y, full(m)) for y, m in zip(up, middle)],
            [fdot(m, full(z)) for z, m in zip(low, middle)],
        )

    upper, lower = lax.fori_loop(0, NS_STEPS - 2, step, (upper, lower))
    middle = [1.5 * eye - 0.5 * fdot(z, full(y)) for y, z in zip(upper, lower)]
    lower = [fdot(m, full(z)) for z, m in zip(lower, middle)]
    return [z * jnp.sqrt(ROWS / s) for z, s in zip(lower, scales)]


def fused_kernel(
    assign, pairing, x_in, out, table, rotated, packed, from_core, from_xy, total, slices, from_z,
    mine_z, gathered, weights,
    core_send, core_recv, xy_send, xy_recv, zr_send, zr_recv, zg_send, zg_recv,
    wxy_send, wxy_recv, wcore_send, wcore_recv,
):
    blk, row = lax.axis_index("blk"), lax.axis_index("row")
    y_lo, z, x = blk // (NZ * NX), lax.rem(blk // NX, NZ), lax.rem(blk, NX)
    y_hi, core = row // 2, lax.rem(row, 2)
    y = y_hi * 2 + y_lo
    half = UNITS // 2

    def device(yy, zz, xx, cc):
        return (lax.rem(yy, 2) * (NZ * NX) + zz * NX + xx, (yy // 2) * 2 + cc)

    def plane(step):
        return lax.rem(y + step // NX, NY), lax.rem(x + lax.rem(step, NX), NX)

    def chunk_to(step):
        yy, xx = plane(step)
        return (yy * NX + xx) * CHUNK

    def chunk_from(step):
        yy, xx = lax.rem(y - step // NX + NY, NY), lax.rem(x - lax.rem(step, NX) + NX, NX)
        return (yy * NX + xx) * CHUNK

    partner = device(y, z, x, 1 - core)

    def plane_device(step):
        yy, xx = plane(step)
        return device(yy, z, xx, core)

    def ring_device(step):
        return device(y, lax.rem(z + step, NZ), x, core)

    def each(first, last, body):
        def run(step, carry):
            body(step)
            return carry

        lax.fori_loop(first, last, run, 0)

    def remote(src, dst, send, recv, to):
        return pltpu.make_async_remote_copy(
            src_ref=src, dst_ref=dst, send_sem=send, recv_sem=recv, device_id=to, device_id_type=MESH
        )

    barrier = pltpu.get_barrier_semaphore()

    def greet(to):
        pl.semaphore_signal(barrier, inc=1, device_id=to, device_id_type=MESH)

    greet(partner)
    each(1, NXY, lambda step: greet(plane_device(step)))
    each(1, NZ, lambda step: greet(ring_device(step)))

    def tile(ct, carry):
        real = x_in[pl.ds(2 * ct, 64, stride=128), :]
        imag = x_in[pl.ds(2 * ct + 1, 64, stride=128), :]
        flipped = jnp.concatenate([real, imag], axis=0).T
        table[pl.ds(4 * ct, 4)] = flipped.reshape(4, BLOCK, 128)
        return carry

    lax.fori_loop(0, BLOCKS // 4, tile, 0, unroll=2)
    pl.semaphore_wait(barrier, NXY + NZ - 1)

    def one_round(rnd, source, target):
        def core_copy(step):
            place = chunk_to(step)
            return remote(
                packed.at[pl.ds((1 - core) * half + place, CHUNK)],
                from_core.at[rnd, pl.ds(place, CHUNK)],
                core_send.at[rnd, step], core_recv.at[rnd, step], partner,
            )

        def xy_copy(step):
            return remote(
                from_core.at[rnd, pl.ds(chunk_to(step), CHUNK)], from_xy.at[rnd, step],
                xy_send.at[rnd, step], xy_recv.at[rnd, step], plane_device(step),
            )

        def gram_units(first):
            for u in range(CHUNK):
                tops = []
                for h in range(2):
                    a, b = pair_places(assign, pairing, rnd, first + u, h)
                    tops.append(gram_top(load_pair(source, a, b)))
                packed[first + u] = pack(*tops)

        def compute(step):
            place = chunk_to(step)
            gram_units((1 - core) * half + place)
            core_copy(step).start()
            gram_units(core * half + place)

        def chunk_sum(step):
            place = chunk_to(step)
            core_copy(step).wait_recv()
            return from_core[rnd, pl.ds(place, CHUNK)] + packed[pl.ds(core * half + place, CHUNK)]

        def ship(step):
            from_core[rnd, pl.ds(chunk_to(step), CHUNK)] = chunk_sum(step)
            xy_copy(step).start()

        def advance(step):
            compute(lax.rem(step, NXY))
            ship(step - 1)

        compute(1)
        each(2, NXY + 1, advance)
        total[...] = chunk_sum(0)

        def add_xy(step):
            xy_copy(step).wait_recv()
            total[...] += from_xy[rnd, step]

        each(1, NXY, add_xy)

        for k in range(NZ):
            slices[k] = total[:, k * SLICE : (k + 1) * SLICE, :]

        def zr_copy(step):
            return remote(
                slices.at[lax.rem(z + step, NZ)], from_z.at[rnd, step],
                zr_send.at[rnd, step], zr_recv.at[rnd, step], ring_device(step),
            )

        def zg_copy(step):
            return remote(
                mine_z, gathered.at[rnd, z], zg_send.at[rnd, step], zg_recv.at[rnd, step],
                ring_device(step),
            )

        def add_zr(step, acc):
            zr_copy(step).wait_recv()
            return acc + from_z[rnd, step]

        each(1, NZ, lambda step: zr_copy(step).start())
        mine_z[...] = lax.fori_loop(1, NZ, add_zr, slices[z])
        gathered[rnd, z] = mine_z[...]
        each(1, NZ, lambda step: zg_copy(step).start())
        each(1, NZ, lambda step: zg_copy(step).wait_recv())

        tops = []
        for u in range(CHUNK):
            tops.extend(unpack(gathered[rnd, :, u].reshape(64, 128)))
        roots = inverse_roots(tops)
        mine = core * half + chunk_to(0)
        for u in range(CHUNK):
            weights[rnd, mine + u] = pack(roots[2 * u], roots[2 * u + 1])

        def wxy_copy(step):
            place = weights.at[rnd, pl.ds(mine, CHUNK)]
            return remote(
                place, place, wxy_send.at[rnd, step], wxy_recv.at[rnd, step], plane_device(step)
            )

        def wcore_copy(step):
            place = weights.at[rnd, pl.ds(core * half + chunk_from(step), CHUNK)]
            return remote(
                place, place, wcore_send.at[rnd, step], wcore_recv.at[rnd, step], partner
            )

        def apply_units(first):
            for u in range(CHUNK):
                d = first + u
                tops = unpack(weights[rnd, d])
                for h in range(2):
                    a, b = pair_places(assign, pairing, rnd, d, h)
                    new = applied(tops[h], load_pair(source, a, b))
                    target[pl.ds(SLOTS * d + 2 * h, 2)] = new.reshape(2, BLOCK, 128)

        def apply_other(step):
            wcore_copy(step).wait_recv()
            apply_units((1 - core) * half + chunk_from(step))

        def take(step):
            wxy_copy(step).wait_recv()
            wcore_copy(step).start()
            apply_units(core * half + chunk_from(step))
            apply_other(step - 1)

        each(1, NXY, lambda step: wxy_copy(step).start())
        wcore_copy(0).start()
        apply_units(mine)
        each(1, NXY, take)
        apply_other(NXY - 1)

        def drain_core(step):
            core_copy(step).wait_send()
            wcore_copy(step).wait_send()

        def drain_xy(step):
            xy_copy(step).wait_send()
            wxy_copy(step).wait_send()

        def drain_z(step):
            zr_copy(step).wait_send()
            zg_copy(step).wait_send()

        each(0, NXY, drain_core)
        each(1, NXY, drain_xy)
        each(1, NZ, drain_z)

    one_round(0, table, rotated)
    one_round(1, rotated, out)


def last_kernel(assign, pairing, source, out, places):
    def place(slot, carry):
        q = lax.rem(slot, SLOTS)
        home = lax.rem(slot // SLOTS - turn_of(q) + UNITS, UNITS)
        places[assign[slot]] = home * SLOTS + position(pairing[1, home], q)
        return carry

    lax.fori_loop(0, BLOCKS, place, 0, unroll=8)

    def tile(ct, carry):
        parts = [source[places[4 * ct + k]] for k in range(4)]
        flipped = jnp.concatenate(parts, axis=0).T
        out[pl.ds(2 * ct, 64, stride=128), :] = flipped[:64]
        out[pl.ds(2 * ct + 1, 64, stride=128), :] = flipped[64:]
        return carry

    lax.fori_loop(0, BLOCKS // 4, tile, 0, unroll=2)


SMEM = pl.BlockSpec(memory_space=pltpu.SMEM)
VMEM = pl.BlockSpec(memory_space=pltpu.VMEM)
TABLE = (BLOCKS, BLOCK, 128)


def rounds(assignment, pairing, x):
    dma = pltpu.SemaphoreType.DMA
    plane, ring = dma((2, NXY)), dma((2, NZ))
    return pl.pallas_call(
        fused_kernel,
        out_shape=jax.ShapeDtypeStruct(TABLE, F32),
        in_specs=[SMEM, SMEM, VMEM],
        out_specs=VMEM,
        scratch_shapes=[
            pltpu.VMEM(TABLE, F32),
            pltpu.VMEM(TABLE, F32),
            pltpu.VMEM((UNITS, 64, 128), F32),
            pltpu.VMEM((2, UNITS // 2, 64, 128), F32),
            pltpu.VMEM((2, NXY, CHUNK, 64, 128), F32),
            pltpu.VMEM((CHUNK, 64, 128), F32),
            pltpu.VMEM((NZ, CHUNK, SLICE, 128), F32),
            pltpu.VMEM((2, NZ, CHUNK, SLICE, 128), F32),
            pltpu.VMEM((CHUNK, SLICE, 128), F32),
            pltpu.VMEM((2, NZ, CHUNK, SLICE, 128), F32),
            pltpu.VMEM((2, UNITS, 64, 128), F32),
            plane, plane, plane, plane, ring, ring, ring, ring, plane, plane, plane, plane,
        ],
        compiler_params=PARAMS(collective_id=0, has_side_effects=True),
        name="rounds",
    )(assignment, pairing, x)


def on_device(transmission, assignment, pairing):
    rows, _, cols = transmission.shape
    x = transmission.reshape(rows, 2, cols // 128, 128).transpose(0, 2, 1, 3).reshape(-1, 128)
    turned_blocks = rounds(assignment, pairing, x)
    out = pl.pallas_call(
        last_kernel,
        out_shape=jax.ShapeDtypeStruct(x.shape, F32),
        in_specs=[SMEM, SMEM, VMEM],
        out_specs=VMEM,
        scratch_shapes=[pltpu.SMEM((BLOCKS,), jnp.int32)],
        compiler_params=PARAMS(),
        name="unturn",
    )(assignment, pairing, turned_blocks)
    out = out.reshape(rows, cols // 128, 2, 128).transpose(0, 2, 1, 3)
    return out.reshape(rows, 2, cols)


def solution(mesh):
    placed = (P(("blk", "row"), None, None), P(), P())
    return jax.shard_map(
        on_device,
        mesh=mesh,
        in_specs=placed,
        out_specs=P(("blk", "row"), None, None),
        check_vma=False,
    )
```

time: 673 us -> 143 us (0.21); the launches traced: 664 us -> 142 us
  local copies, waits for them, and re-layouts: 292 us -> 0 us
  waiting for transfers between devices: 227 us -> 0 us
  Pallas kernels: 0 us -> 142 us
  other arithmetic: 49.8 us -> 0 us
  matrix products: 44.1 us -> 0 us
  starting transfers between devices: 30.1 us -> 0 us
  between operations: 21.6 us -> 0.01 us
    gather x10 -> x0, local copies, waits for them, and re-layouts: 159 us -> none  [the longest x1 58.2 us: on_device(): outgoing = jnp.take(flat, column_index(held, total_cols), axis=1)]
    pallas_call x0 -> x2, Pallas kernels: none -> 142 us  [the longest x1 129 us: rounds(): pl.pallas_call(fused_kernel, out_shape=jax.ShapeDtypeStruct(TABLE, F32),...]
    all_to_all x2 -> x0, waiting for transfers between devices: 117 us -> none  [the longest x1 85.1 us: on_device(): lax.all_to_all(outgoing, 'blk', split_axis=1, concat_axis=0, tiled=True)]
    psum x2 -> x0, waiting for transfers between devices: 88.2 us -> none  [summed_pair(): gram = lax.psum(local_gram(joined), 'row')]
    scatter x5 -> x0, local copies, waits for them, and re-layouts: 74.3 us -> none  [the longest x3 63.5 us: inverse_of(): jnp.zeros(index.shape, jnp.int32).at[index]]
    dot_general x76 -> x0, matrix products: 44.1 us -> none  [the longest x4 15.1 us: local_gram(): return jnp.dot(joined.T, joined, precision=lax.Precision.HIGHEST)]
    select_n x13 -> x0, other arithmetic: 37.5 us -> none  [the longest x1 13.1 us: on_device(): outgoing = jnp.take(flat, column_index(held, total_cols), axis=1)]
    all_to_all x2 -> x0, starting transfers between devices: 24.3 us -> none  [the longest x1 13.9 us: on_device(): lax.all_to_all(outgoing, 'blk', split_axis=1, concat_axis=0, tiled=True)]
  transfers between devices with their start and end apart: 6 -> 0, of which waited for: 5 -> 0; matrix products, arithmetic and copies ran while one was open for 11% -> 0% of each run, Pallas kernels for 0% -> 0%
where the time goes in v2:
time: 143 us; the launch traced here: 142 us
  Pallas kernels  142 us (99%)
    pallas_call x1, Pallas kernels, rounds(): pl.pallas_call(fused_kernel, out_shape=jax.ShapeDtypeStruct(TABLE, F32),...  129 us
    pallas_call x1, Pallas kernels, on_device(): pl.pallas_call(last_kernel, out_shape=jax.ShapeDtypeStruct(x.shape, F32),...  13 us

profile of v2, /device:TPU:1, one launch (start us, length us, event | category | flops | bytes accessed | tf_op | source)
XLA Modules:
  0.0 142.2 jit_solution(8063298349431184479)
XLA Ops:
  0.0 129.2 %rounds.1.source = f32[256,32,128]{2,1,0:T(8,128)} custom-call(s32[256]{0:T(256)} %assign.3, s32[2,64]{1,0:T(2,128)} %pairing.3, f32[8192,128]{1,0:T(8,128)} %bitcast.10), custom_call_target="tpu_custom_call" | custom-call | tf_op jit(solution)/shard_map/rounds/pallas_call | solution.py:409
  129.3 13.0 %unturn.1 = f32[8192,128]{1,0:T(8,128)} custom-call(s32[256]{0:T(256)} %assign.3, s32[2,64]{1,0:T(2,128)} %pairing.3, f32[256,32,128]{2,1,0:T(8,128)} %rounds.1.source), custom_call_target="tpu_custom_call" | custom-call | tf_op jit(solution)/shard_map/unturn/pallas_call | solution.py:437

commit v3 on v2

--- a/solution.py
+++ b/solution.py
@@ -171,40 +171,46 @@
     return [z * jnp.sqrt(ROWS / s) for z, s in zip(lower, scales)]
 
 
+def order_in(i):
+    return lax.rem(2 + 3 * i + 3 * (i * (i - 1) // 2), 4)
+
+
+def order_out(i):
+    return lax.rem(3 * i + 3 * (i * (i - 1) // 2), 4)
+
+
 def fused_kernel(
-    assign, pairing, x_in, out, table, rotated, packed, from_core, from_xy, total, slices, from_z,
+    assign, pairing, x_in, out, table, rotated, packed, from_core, relay, inbox, total, slices, from_z,
     mine_z, gathered, weights,
-    core_send, core_recv, xy_send, xy_recv, zr_send, zr_recv, zg_send, zg_recv,
-    wxy_send, wxy_recv, wcore_send, wcore_recv,
+    core_send, core_recv, relay_send, relay_recv, inbox_send, inbox_recv, zr_send, zr_recv, zg_send,
+    zg_recv, wfull_send, wfull_recv, whalf_send, whalf_recv, wcore_send, wcore_recv,
 ):
     blk, row = lax.axis_index("blk"), lax.axis_index("row")
     y_lo, z, x = blk // (NZ * NX), lax.rem(blk // NX, NZ), lax.rem(blk, NX)
     y_hi, core = row // 2, lax.rem(row, 2)
     y = y_hi * 2 + y_lo
     half = UNITS // 2
+    p, q = x + core * (y - x), y + core * (x - y)
 
     def device(yy, zz, xx, cc):
         return (lax.rem(yy, 2) * (NZ * NX) + zz * NX + xx, (yy // 2) * 2 + cc)
 
-    def plane(step):
-        return lax.rem(y + step // NX, NY), lax.rem(x + lax.rem(step, NX), NX)
-
-    def chunk_to(step):
-        yy, xx = plane(step)
-        return (yy * NX + xx) * CHUNK
-
-    def chunk_from(step):
-        yy, xx = lax.rem(y - step // NX + NY, NY), lax.rem(x - lax.rem(step, NX) + NX, NX)
-        return (yy * NX + xx) * CHUNK
+    def beside(direction, second):
+        move = 1 + 2 * direction
+        pp = lax.rem(p + move * (1 - second), 4)
+        qq = lax.rem(q + move * second, 4)
+        return device(qq + core * (pp - qq), z, pp + core * (qq - pp), core)
 
     partner = device(y, z, x, 1 - core)
-
-    def plane_device(step):
-        yy, xx = plane(step)
-        return device(yy, z, xx, core)
 
     def ring_device(step):
         return device(y, lax.rem(z + step, NZ), x, core)
+
+    def my_chunk(da, db):
+        return (lax.rem(p + da, 4) * 4 + lax.rem(q + db, 4)) * CHUNK
+
+    def other_chunk(da, db):
+        return (lax.rem(q + da, 4) * 4 + lax.rem(p + db, 4)) * CHUNK
 
     def each(first, last, body):
         def run(step, carry):
@@ -224,7 +230,9 @@
         pl.semaphore_signal(barrier, inc=1, device_id=to, device_id_type=MESH)
 
     greet(partner)
-    each(1, NXY, lambda step: greet(plane_device(step)))
+    for direction in range(2):
+        for second in range(2):
+            greet(beside(direction, second))
     each(1, NZ, lambda step: greet(ring_device(step)))
 
     def tile(ct, carry):
@@ -235,21 +243,29 @@
         return carry
 
     lax.fori_loop(0, BLOCKS // 4, tile, 0, unroll=2)
-    pl.semaphore_wait(barrier, NXY + NZ - 1)
+    pl.semaphore_wait(barrier, 4 + NZ)
 
     def one_round(rnd, source, target):
         def core_copy(step):
-            place = chunk_to(step)
+            place = other_chunk(order_in(step // 4), order_in(lax.rem(step, 4)))
             return remote(
                 packed.at[pl.ds((1 - core) * half + place, CHUNK)],
                 from_core.at[rnd, pl.ds(place, CHUNK)],
                 core_send.at[rnd, step], core_recv.at[rnd, step], partner,
             )
 
-        def xy_copy(step):
-            return remote(
-                from_core.at[rnd, pl.ds(chunk_to(step), CHUNK)], from_xy.at[rnd, step],
-                xy_send.at[rnd, step], xy_recv.at[rnd, step], plane_device(step),
+        def relay_copy(direction, slot, place, second):
+            return remote(
+                from_core.at[rnd, place + direction], relay.at[rnd, direction, slot],
+                relay_send.at[rnd, direction, slot], relay_recv.at[rnd, direction, slot],
+                beside(direction, second),
+            )
+
+        def inbox_copy(direction, slot, place, second):
+            return remote(
+                from_core.at[rnd, pl.ds(place, CHUNK)], inbox.at[rnd, direction, slot],
+                inbox_send.at[rnd, direction, slot], inbox_recv.at[rnd, direction, slot],
+                beside(direction, second),
             )
 
         def gram_units(first):
@@ -261,33 +277,56 @@
                 packed[first + u] = pack(*tops)
 
         def compute(step):
-            place = chunk_to(step)
-            gram_units((1 - core) * half + place)
+            da, db = order_in(step // 4), order_in(lax.rem(step, 4))
+            gram_units((1 - core) * half + other_chunk(da, db))
             core_copy(step).start()
-            gram_units(core * half + place)
-
-        def chunk_sum(step):
-            place = chunk_to(step)
+            gram_units(core * half + my_chunk(da, db))
+
+        def inbox_sum(slot):
+            for direction in range(2):
+                inbox_copy(direction, slot, 0, 0).wait_recv()
+            return inbox[rnd, 0, slot] + inbox[rnd, 1, slot]
+
+        def ship(step):
+            ia, ib = step // 4, lax.rem(step, 4)
+            second = step // 12
+            kind, slot = ia + second * (ib - ia), ib + second * (4 - ib)
+            place = my_chunk(order_in(ia), order_in(ib))
+            chunk = pl.ds(place, CHUNK)
             core_copy(step).wait_recv()
-            return from_core[rnd, pl.ds(place, CHUNK)] + packed[pl.ds(core * half + place, CHUNK)]
-
-        def ship(step):
-            from_core[rnd, pl.ds(chunk_to(step), CHUNK)] = chunk_sum(step)
-            xy_copy(step).start()
+            from_core[rnd, chunk] += packed[pl.ds(core * half + place, CHUNK)]
+
+            @pl.when(second == 1)
+            def _():
+                from_core[rnd, chunk] += inbox_sum(ib)
+
+            @pl.when(kind == 0)
+            def _():
+                for direction in range(2):
+                    relay_copy(direction, slot, place, second).start()
+
+            for direction in range(2):
+
+                @pl.when(kind == 1 + direction)
+                def _(direction=direction):
+                    relay_copy(direction, slot, place, second).wait_recv()
+                    from_core[rnd, place + direction] += relay[rnd, direction, slot]
+                    inbox_copy(direction, slot, place, second).start()
 
         def advance(step):
-            compute(lax.rem(step, NXY))
+            compute(step)
             ship(step - 1)
 
-        compute(1)
-        each(2, NXY + 1, advance)
-        total[...] = chunk_sum(0)
-
-        def add_xy(step):
-            xy_copy(step).wait_recv()
-            total[...] += from_xy[rnd, step]
-
-        each(1, NXY, add_xy)
+        compute(0)
+        each(1, 16, advance)
+        core_copy(15).wait_recv()
+        place = my_chunk(0, 0)
+        total[...] = (
+            from_core[rnd, pl.ds(place, CHUNK)]
+            + packed[pl.ds(core * half + place, CHUNK)]
+            + inbox_sum(3)
+            + inbox_sum(4)
+        )
 
         for k in range(NZ):
             slices[k] = total[:, k * SLICE : (k + 1) * SLICE, :]
@@ -304,34 +343,52 @@
                 ring_device(step),
             )
 
-        def add_zr(step, acc):
+        far_first = (4, 3, 5, 2, 6, 1, 7)
+        for step in far_first:
+            zr_copy(step).start()
+        acc = slices[z]
+        for step in reversed(far_first):
             zr_copy(step).wait_recv()
-            return acc + from_z[rnd, step]
-
-        each(1, NZ, lambda step: zr_copy(step).start())
-        mine_z[...] = lax.fori_loop(1, NZ, add_zr, slices[z])
-        gathered[rnd, z] = mine_z[...]
-        each(1, NZ, lambda step: zg_copy(step).start())
-        each(1, NZ, lambda step: zg_copy(step).wait_recv())
+            acc = acc + from_z[rnd, step]
+        mine_z[...] = acc
+        for step in far_first:
+            zg_copy(step).start()
+        gathered[rnd, z] = acc
+        for step in reversed(far_first):
+            zg_copy(step).wait_recv()
 
         tops = []
         for u in range(CHUNK):
             tops.extend(unpack(gathered[rnd, :, u].reshape(64, 128)))
         roots = inverse_roots(tops)
-        mine = core * half + chunk_to(0)
+        mine = core * half + place
         for u in range(CHUNK):
             weights[rnd, mine + u] = pack(roots[2 * u], roots[2 * u + 1])
 
-        def wxy_copy(step):
-            place = weights.at[rnd, pl.ds(mine, CHUNK)]
-            return remote(
-                place, place, wxy_send.at[rnd, step], wxy_recv.at[rnd, step], plane_device(step)
-            )
+        def wfull_copy(direction, slot, first, second):
+            part = weights.at[rnd, pl.ds(first, CHUNK)]
+            return remote(
+                part, part, wfull_send.at[rnd, direction, slot], wfull_recv.at[rnd, direction, slot],
+                beside(direction, second),
+            )
+
+        def whalf_copy(direction, slot, first, second):
+            part = weights.at[rnd, first + direction]
+            return remote(
+                part, part, whalf_send.at[rnd, direction, slot], whalf_recv.at[rnd, direction, slot],
+                beside(direction, second),
+            )
+
+        def my_units(step):
+            return core * half + my_chunk(order_out(step // 4), order_out(lax.rem(step, 4)))
+
+        def other_units(step):
+            return (1 - core) * half + other_chunk(order_out(step // 4), order_out(lax.rem(step, 4)))
 
         def wcore_copy(step):
-            place = weights.at[rnd, pl.ds(core * half + chunk_from(step), CHUNK)]
-            return remote(
-                place, place, wcore_send.at[rnd, step], wcore_recv.at[rnd, step], partner
+            part = weights.at[rnd, pl.ds(my_units(step), CHUNK)]
+            return remote(
+                part, part, wcore_send.at[rnd, step], wcore_recv.at[rnd, step], partner
             )
 
         def apply_units(first):
@@ -345,57 +402,93 @@
 
         def apply_other(step):
             wcore_copy(step).wait_recv()
-            apply_units((1 - core) * half + chunk_from(step))
+            apply_units(other_units(step))
 
         def take(step):
-            wxy_copy(step).wait_recv()
+            ia, ib = step // 4, lax.rem(step, 4)
+            second = (15 - step) // 12
+            kind, slot = ia + second * (ib - ia), ib + second * (4 - ib)
+            first = my_units(step)
+            for direction in range(2):
+
+                @pl.when(kind == 1 + direction)
+                def _(direction=direction):
+                    wfull_copy(direction, slot, first, second).wait_recv()
+                    whalf_copy(direction, slot, first, second).start()
+
+            @pl.when(kind == 3)
+            def _():
+                for direction in range(2):
+                    whalf_copy(direction, slot, first, second).wait_recv()
+
+            @pl.when(second == 1)
+            def _():
+                for direction in range(2):
+                    wfull_copy(direction, ib, first, 0).start()
+
             wcore_copy(step).start()
-            apply_units(core * half + chunk_from(step))
+            apply_units(first)
             apply_other(step - 1)
 
-        each(1, NXY, lambda step: wxy_copy(step).start())
+        for direction in range(2):
+            wfull_copy(direction, 4, mine, 1).start()
+        for direction in range(2):
+            wfull_copy(direction, 0, mine, 0).start()
         wcore_copy(0).start()
         apply_units(mine)
-        each(1, NXY, take)
-        apply_other(NXY - 1)
+        each(1, 16, take)
+        apply_other(15)
 
         def drain_core(step):
             core_copy(step).wait_send()
             wcore_copy(step).wait_send()
 
-        def drain_xy(step):
-            xy_copy(step).wait_send()
-            wxy_copy(step).wait_send()
+        def drain_plane(slot):
+            for direction in range(2):
+                relay_copy(direction, slot, 0, 0).wait_send()
+                inbox_copy(direction, slot, 0, 0).wait_send()
+                wfull_copy(direction, slot, 0, 0).wait_send()
+                whalf_copy(direction, slot, 0, 0).wait_send()
 
         def drain_z(step):
             zr_copy(step).wait_send()
             zg_copy(step).wait_send()
 
-        each(0, NXY, drain_core)
-        each(1, NXY, drain_xy)
+        each(0, 16, drain_core)
+        each(0, 5, drain_plane)
         each(1, NZ, drain_z)
 
     one_round(0, table, rotated)
     one_round(1, rotated, out)
 
 
+STEP = 8
+
+
 def last_kernel(assign, pairing, source, out, places):
-    def place(slot, carry):
-        q = lax.rem(slot, SLOTS)
-        home = lax.rem(slot // SLOTS - turn_of(q) + UNITS, UNITS)
-        places[assign[slot]] = home * SLOTS + position(pairing[1, home], q)
-        return carry
-
-    lax.fori_loop(0, BLOCKS, place, 0, unroll=8)
-
-    def tile(ct, carry):
-        parts = [source[places[4 * ct + k]] for k in range(4)]
+    @pl.when(pl.program_id(0) == 0)
+    def _():
+        def unit(d, carry):
+            up = jnp.where(d == UNITS - 1, 0, d + 1)
+            down = jnp.where(d == 0, UNITS - 1, d - 1)
+            here, above, below = pairing[1, d], pairing[1, up], pairing[1, down]
+            places[assign[SLOTS * d]] = SLOTS * d
+            places[assign[SLOTS * d + 1]] = SLOTS * up + jnp.where(above == 0, 1, 2)
+            places[assign[SLOTS * d + 2]] = SLOTS * down + jnp.where(
+                below == 0, 2, jnp.where(below == 1, 1, 3)
+            )
+            places[assign[SLOTS * d + 3]] = SLOTS * d + jnp.where(here == 2, 1, 3)
+            return carry
+
+        lax.fori_loop(0, UNITS, unit, 0, unroll=4)
+
+    flat = out.reshape(64 * 2 * STEP, 128)
+    for k in range(STEP):
+        ct = pl.program_id(0) * STEP + k
+        parts = [source[places[4 * ct + j]] for j in range(4)]
         flipped = jnp.concatenate(parts, axis=0).T
-        out[pl.ds(2 * ct, 64, stride=128), :] = flipped[:64]
-        out[pl.ds(2 * ct + 1, 64, stride=128), :] = flipped[64:]
-        return carry
-
-    lax.fori_loop(0, BLOCKS // 4, tile, 0, unroll=2)
+        flat[pl.ds(2 * k, 64, stride=2 * STEP), :] = flipped[:64]
+        flat[pl.ds(2 * k + 1, 64, stride=2 * STEP), :] = flipped[64:]
 
 
 SMEM = pl.BlockSpec(memory_space=pltpu.SMEM)
@@ -405,7 +498,7 @@
 
 def rounds(assignment, pairing, x):
     dma = pltpu.SemaphoreType.DMA
-    plane, ring = dma((2, NXY)), dma((2, NZ))
+    chunks, plane, ring = dma((2, 16)), dma((2, 2, 5)), dma((2, NZ))
     return pl.pallas_call(
         fused_kernel,
         out_shape=jax.ShapeDtypeStruct(TABLE, F32),
@@ -416,33 +509,41 @@
             pltpu.VMEM(TABLE, F32),
             pltpu.VMEM((UNITS, 64, 128), F32),
             pltpu.VMEM((2, UNITS // 2, 64, 128), F32),
-            pltpu.VMEM((2, NXY, CHUNK, 64, 128), F32),
+            pltpu.VMEM((2, 2, 5, 64, 128), F32),
+            pltpu.VMEM((2, 2, 5, CHUNK, 64, 128), F32),
             pltpu.VMEM((CHUNK, 64, 128), F32),
             pltpu.VMEM((NZ, CHUNK, SLICE, 128), F32),
             pltpu.VMEM((2, NZ, CHUNK, SLICE, 128), F32),
             pltpu.VMEM((CHUNK, SLICE, 128), F32),
             pltpu.VMEM((2, NZ, CHUNK, SLICE, 128), F32),
             pltpu.VMEM((2, UNITS, 64, 128), F32),
-            plane, plane, plane, plane, ring, ring, ring, ring, plane, plane, plane, plane,
+            chunks, chunks, plane, plane, plane, plane, ring, ring, ring, ring,
+            plane, plane, plane, plane, chunks, chunks,
         ],
         compiler_params=PARAMS(collective_id=0, has_side_effects=True),
         name="rounds",
     )(assignment, pairing, x)
 
 
+def unturned(assignment, pairing, source):
+    shape = (64, BLOCKS // 2, 128)
+    return pl.pallas_call(
+        last_kernel,
+        out_shape=jax.ShapeDtypeStruct(shape, F32),
+        grid=(BLOCKS // 4 // STEP,),
+        in_specs=[SMEM, SMEM, VMEM],
+        out_specs=pl.BlockSpec((64, 2 * STEP, 128), lambda i: (0, i, 0)),
+        scratch_shapes=[pltpu.SMEM((BLOCKS,), jnp.int32)],
+        compiler_params=PARAMS(),
+        name="unturn",
+    )(assignment, pairing, source)
+
+
 def on_device(transmission, assignment, pairing):
     rows, _, cols = transmission.shape
     x = transmission.reshape(rows, 2, cols // 128, 128).transpose(0, 2, 1, 3).reshape(-1, 128)
     turned_blocks = rounds(assignment, pairing, x)
-    out = pl.pallas_call(
-        last_kernel,
-        out_shape=jax.ShapeDtypeStruct(x.shape, F32),
-        in_specs=[SMEM, SMEM, VMEM],
-        out_specs=VMEM,
-        scratch_shapes=[pltpu.SMEM((BLOCKS,), jnp.int32)],
-        compiler_params=PARAMS(),
-        name="unturn",
-    )(assignment, pairing, turned_blocks)
+    out = unturned(assignment, pairing, turned_blocks)
     out = out.reshape(rows, cols // 128, 2, 128).transpose(0, 2, 1, 3)
     return out.reshape(rows, 2, cols)
 

time: 143 us -> 134 us (0.937)
  Pallas kernels: 142 us -> 133 us
    pallas_call x1, Pallas kernels: 13 us -> 7.72 us  [unturned(): pl.pallas_call(last_kernel, out_shape=jax.ShapeDtypeStruct(shape, F32), g...]
    pallas_call x1, Pallas kernels: 129 us -> 126 us  [rounds(): pl.pallas_call(fused_kernel, out_shape=jax.ShapeDtypeStruct(TABLE, F32),...]
where the time goes in v3:
time: 134 us; the launch traced here: 133 us
  Pallas kernels  133 us (99%)
    pallas_call x1, Pallas kernels, rounds(): pl.pallas_call(fused_kernel, out_shape=jax.ShapeDtypeStruct(TABLE, F32),...  126 us
    pallas_call x1, Pallas kernels, unturned(): pl.pallas_call(last_kernel, out_shape=jax.ShapeDtypeStruct(shape, F32), g...  7.72 us

profile of v3, /device:TPU:1, one launch (start us, length us, event | category | flops | bytes accessed | tf_op | source)
XLA Modules:
  0.0 133.4 jit_solution(666296834197689652)
XLA Ops:
  0.0 125.7 %rounds.1.source = f32[256,32,128]{2,1,0:T(8,128)} custom-call(s32[256]{0:T(256)} %assign.3, s32[2,64]{1,0:T(2,128)} %pairing.3, f32[8192,128]{1,0:T(8,128)} %bitcast.10), custom_call_target="tpu_custom_call" | custom-call | tf_op jit(solution)/shard_map/rounds/pallas_call | solution.py:502
  125.7 7.7 %unturn.1 = f32[64,128,128]{2,1,0:T(8,128)} custom-call(s32[256]{0:T(256)} %assign.3, s32[2,64]{1,0:T(2,128)} %pairing.3, f32[256,32,128]{2,1,0:T(8,128)} %rounds.1.source), custom_call_target="tpu_custom_call" | custom-call | tf_op jit(solution)/shard_map/unturn/pallas_call | solution.py:530

commit v4 on v3

--- a/solution.py
+++ b/solution.py
@@ -20,7 +20,9 @@
 NXY = NX * NY
 CHUNK = UNITS // 2 // NXY
 SLICE = 64 // NZ
-PARAMS = functools.partial(pltpu.CompilerParams, vmem_limit_bytes=56 * 1024 * 1024)
+STEP = 8
+GROUPS = BLOCKS // 4 // STEP
+PARAMS = functools.partial(pltpu.CompilerParams, vmem_limit_bytes=60 * 1024 * 1024)
 
 
 def position(pick, slot):
@@ -87,28 +89,31 @@
 def pack(first, second):
     lane, row = lanes_of(first.shape), rows_of(first.shape)
     left = lane < 64
-    packed_first = jnp.where(row <= lane, first, pltpu.roll(first, 64, 1))
-    packed_second = jnp.where(row <= lane - 64, pltpu.roll(second, 64, 1), second)
-    return jnp.where(left, packed_first, packed_second)
-
-
-def both(pair):
-    return jnp.concatenate([pair, turned(pair)], axis=0)
+    real = jnp.where(left, first, second)
+    imag = pltpu.roll(jnp.where(left, second, first), 64, 1)
+    return jnp.where(row <= jnp.where(left, lane, lane - 64), real, imag)
 
 
 def nt_dot(a, b):
     return lax.dot_general(a, b, (((1,), (1,)), ((), ())), preferred_element_type=F32)
 
 
-def gram_top(pair):
-    high, low = split(both(pair))
-    lhs = jnp.concatenate([high[:64], low[:64]], axis=1)
+def parts_of(table, a, b, swapped=False):
+    order = (1, 0) if swapped else (0, 1)
+    return jnp.concatenate([table[k, half] for half in order for k in (a, b)], axis=0)
+
+
+def gram_top(tables, a, b, swapped):
+    high = parts_of(tables[0], a, b, swapped)
+    low = parts_of(tables[1], a, b, swapped)
+    pair = slice(64, 128) if swapped else slice(0, 64)
+    lhs = jnp.concatenate([high[pair], low[pair]], axis=1)
     rhs = jnp.concatenate([high, high], axis=1)
-    return nt_dot(lhs, rhs) + nt_dot(high[:64], low)
-
-
-def applied(top, pair):
-    high, low = split(both(pair))
+    return nt_dot(lhs, rhs) + nt_dot(high[pair], low)
+
+
+def applied(top, tables, a, b):
+    high, low = parts_of(tables[0], a, b), parts_of(tables[1], a, b)
     whigh, wlow = split(top)
     lhs = jnp.concatenate([whigh, wlow], axis=1)
     rhs = jnp.concatenate([high, high], axis=0)
@@ -117,8 +122,10 @@
     )
 
 
-def load_pair(table, a, b):
-    return jnp.concatenate([table[a], table[b]], axis=0)
+def keep(tables, first, count, value):
+    for index, whole in enumerate((value, turned(value))):
+        for table, part in zip(tables, split(whole)):
+            table[pl.ds(first, count), index] = part.reshape(count, BLOCK, 128)
 
 
 def full(top):
@@ -180,10 +187,11 @@
 
 
 def fused_kernel(
-    assign, pairing, x_in, out, table, rotated, packed, from_core, relay, inbox, total, slices, from_z,
-    mine_z, gathered, weights,
-    core_send, core_recv, relay_send, relay_recv, inbox_send, inbox_recv, zr_send, zr_recv, zg_send,
-    zg_recv, wfull_send, wfull_recv, whalf_send, whalf_recv, wcore_send, wcore_recv,
+    assign, pairing, x_in, out, x_held, results, high0, low0, high1, low1, packed, from_core, relay,
+    inbox, second_in, total, slices, from_z, mine_z, gathered, weights, x_sem, out_sem,
+    core_send, core_recv, relay_send, relay_recv, inbox_send, inbox_recv, second_send, second_recv, zr_send,
+    zr_recv, zg_send, zg_recv, wfull_send, wfull_recv, whalf_send, whalf_recv, wsecond_send,
+    wsecond_recv, wcore_send, wcore_recv,
 ):
     blk, row = lax.axis_index("blk"), lax.axis_index("row")
     y_lo, z, x = blk // (NZ * NX), lax.rem(blk // NX, NZ), lax.rem(blk, NX)
@@ -195,11 +203,14 @@
     def device(yy, zz, xx, cc):
         return (lax.rem(yy, 2) * (NZ * NX) + zz * NX + xx, (yy // 2) * 2 + cc)
 
-    def beside(direction, second):
-        move = 1 + 2 * direction
-        pp = lax.rem(p + move * (1 - second), 4)
-        qq = lax.rem(q + move * second, 4)
+    def placed(pp, qq):
         return device(qq + core * (pp - qq), z, pp + core * (qq - pp), core)
+
+    def beside(direction):
+        return placed(lax.rem(p + 1 + 2 * direction, 4), q)
+
+    def across(distance):
+        return placed(p, lax.rem(q + distance, 4))
 
     partner = device(y, z, x, 1 - core)
 
@@ -231,21 +242,31 @@
 
     greet(partner)
     for direction in range(2):
-        for second in range(2):
-            greet(beside(direction, second))
-    each(1, NZ, lambda step: greet(ring_device(step)))
-
-    def tile(ct, carry):
-        real = x_in[pl.ds(2 * ct, 64, stride=128), :]
-        imag = x_in[pl.ds(2 * ct + 1, 64, stride=128), :]
-        flipped = jnp.concatenate([real, imag], axis=0).T
-        table[pl.ds(4 * ct, 4)] = flipped.reshape(4, BLOCK, 128)
-        return carry
-
-    lax.fori_loop(0, BLOCKS // 4, tile, 0, unroll=2)
-    pl.semaphore_wait(barrier, 4 + NZ)
-
-    def one_round(rnd, source, target):
+        greet(beside(direction))
+    for distance in range(1, 4):
+        greet(across(distance))
+    for step in range(1, NZ):
+        greet(ring_device(step))
+
+    def x_copy(group):
+        return pltpu.make_async_copy(
+            x_in.at[:, pl.ds(group * 2 * STEP, 2 * STEP)], x_held.at[group], x_sem.at[group]
+        )
+
+    def load_group(group):
+        x_copy(group).wait()
+        flat = x_held.at[group].reshape(64 * 2 * STEP, 128)
+        for k in range(STEP):
+            real = flat[pl.ds(2 * k, 64, stride=2 * STEP), :]
+            imag = flat[pl.ds(2 * k + 1, 64, stride=2 * STEP), :]
+            flipped = jnp.concatenate([real, imag], axis=0).T
+            keep((high0, low0), 4 * (group * STEP + k), 4, flipped)
+
+    each(0, GROUPS, lambda group: x_copy(group).start())
+    each(0, GROUPS, load_group)
+    pl.semaphore_wait(barrier, 6 + NZ - 1)
+
+    def one_round(rnd, source):
         def core_copy(step):
             place = other_chunk(order_in(step // 4), order_in(lax.rem(step, 4)))
             return remote(
@@ -254,18 +275,24 @@
                 core_send.at[rnd, step], core_recv.at[rnd, step], partner,
             )
 
-        def relay_copy(direction, slot, place, second):
+        def relay_copy(direction, slot, place):
             return remote(
                 from_core.at[rnd, place + direction], relay.at[rnd, direction, slot],
                 relay_send.at[rnd, direction, slot], relay_recv.at[rnd, direction, slot],
-                beside(direction, second),
-            )
-
-        def inbox_copy(direction, slot, place, second):
+                beside(direction),
+            )
+
+        def inbox_copy(direction, slot, place):
             return remote(
                 from_core.at[rnd, pl.ds(place, CHUNK)], inbox.at[rnd, direction, slot],
                 inbox_send.at[rnd, direction, slot], inbox_recv.at[rnd, direction, slot],
-                beside(direction, second),
+                beside(direction),
+            )
+
+        def second_copy(ib, place):
+            return remote(
+                from_core.at[rnd, pl.ds(place, CHUNK)], second_in.at[rnd, ib],
+                second_send.at[rnd, ib], second_recv.at[rnd, ib], across(order_in(ib)),
             )
 
         def gram_units(first):
@@ -273,7 +300,7 @@
                 tops = []
                 for h in range(2):
                     a, b = pair_places(assign, pairing, rnd, first + u, h)
-                    tops.append(gram_top(load_pair(source, a, b)))
+                    tops.append(gram_top(source, a, b, h == 1))
                 packed[first + u] = pack(*tops)
 
         def compute(step):
@@ -284,34 +311,33 @@
 
         def inbox_sum(slot):
             for direction in range(2):
-                inbox_copy(direction, slot, 0, 0).wait_recv()
+                inbox_copy(direction, slot, 0).wait_recv()
             return inbox[rnd, 0, slot] + inbox[rnd, 1, slot]
 
         def ship(step):
             ia, ib = step // 4, lax.rem(step, 4)
-            second = step // 12
-            kind, slot = ia + second * (ib - ia), ib + second * (4 - ib)
             place = my_chunk(order_in(ia), order_in(ib))
             chunk = pl.ds(place, CHUNK)
             core_copy(step).wait_recv()
             from_core[rnd, chunk] += packed[pl.ds(core * half + place, CHUNK)]
 
-            @pl.when(second == 1)
+            @pl.when(ia == 0)
+            def _():
+                for direction in range(2):
+                    relay_copy(direction, ib, place).start()
+
+            for direction in range(2):
+
+                @pl.when(ia == 1 + direction)
+                def _(direction=direction):
+                    relay_copy(direction, ib, place).wait_recv()
+                    from_core[rnd, place + direction] += relay[rnd, direction, ib]
+                    inbox_copy(direction, ib, place).start()
+
+            @pl.when(ia == 3)
             def _():
                 from_core[rnd, chunk] += inbox_sum(ib)
-
-            @pl.when(kind == 0)
-            def _():
-                for direction in range(2):
-                    relay_copy(direction, slot, place, second).start()
-
-            for direction in range(2):
-
-                @pl.when(kind == 1 + direction)
-                def _(direction=direction):
-                    relay_copy(direction, slot, place, second).wait_recv()
-                    from_core[rnd, place + direction] += relay[rnd, direction, slot]
-                    inbox_copy(direction, slot, place, second).start()
+                second_copy(ib, place).start()
 
         def advance(step):
             compute(step)
@@ -325,8 +351,10 @@
             from_core[rnd, pl.ds(place, CHUNK)]
             + packed[pl.ds(core * half + place, CHUNK)]
             + inbox_sum(3)
-            + inbox_sum(4)
         )
+        for ib in range(3):
+            second_copy(ib, 0).wait_recv()
+            total[...] += second_in[rnd, ib]
 
         for k in range(NZ):
             slices[k] = total[:, k * SLICE : (k + 1) * SLICE, :]
@@ -363,20 +391,27 @@
         roots = inverse_roots(tops)
         mine = core * half + place
         for u in range(CHUNK):
-            weights[rnd, mine + u] = pack(roots[2 * u], roots[2 * u + 1])
-
-        def wfull_copy(direction, slot, first, second):
+            weights[rnd, mine + u] = pack(roots[2 * u], pltpu.roll(roots[2 * u + 1], 64, 1))
+
+        def wfull_copy(direction, slot, first):
             part = weights.at[rnd, pl.ds(first, CHUNK)]
             return remote(
                 part, part, wfull_send.at[rnd, direction, slot], wfull_recv.at[rnd, direction, slot],
-                beside(direction, second),
-            )
-
-        def whalf_copy(direction, slot, first, second):
+                beside(direction),
+            )
+
+        def whalf_copy(direction, slot, first):
             part = weights.at[rnd, first + direction]
             return remote(
                 part, part, whalf_send.at[rnd, direction, slot], whalf_recv.at[rnd, direction, slot],
-                beside(direction, second),
+                beside(direction),
+            )
+
+        def wsecond_copy(ib, first):
+            part = weights.at[rnd, pl.ds(first, CHUNK)]
+            return remote(
+                part, part, wsecond_send.at[rnd, ib], wsecond_recv.at[rnd, ib],
+                across(4 - order_out(ib)),
             )
 
         def my_units(step):
@@ -391,78 +426,93 @@
                 part, part, wcore_send.at[rnd, step], wcore_recv.at[rnd, step], partner
             )
 
-        def apply_units(first):
+        def out_copy(first, which):
+            place = pl.ds(SLOTS * first, SLOTS * CHUNK)
+            return pltpu.make_async_copy(results.at[place], out.at[place], out_sem.at[which])
+
+        def apply_units(first, which):
             for u in range(CHUNK):
                 d = first + u
                 tops = unpack(weights[rnd, d])
                 for h in range(2):
                     a, b = pair_places(assign, pairing, rnd, d, h)
-                    new = applied(tops[h], load_pair(source, a, b))
-                    target[pl.ds(SLOTS * d + 2 * h, 2)] = new.reshape(2, BLOCK, 128)
+                    new = applied(tops[h], source, a, b)
+                    place = SLOTS * d + 2 * h
+                    if rnd == 0:
+                        keep((high1, low1), place, 2, new)
+                    else:
+                        results[pl.ds(place, 2)] = new.reshape(2, BLOCK, 128)
+            if rnd == 1:
+                out_copy(first, which).start()
 
         def apply_other(step):
             wcore_copy(step).wait_recv()
-            apply_units(other_units(step))
+            apply_units(other_units(step), 16 + step)
 
         def take(step):
             ia, ib = step // 4, lax.rem(step, 4)
-            second = (15 - step) // 12
-            kind, slot = ia + second * (ib - ia), ib + second * (4 - ib)
             first = my_units(step)
+
+            @pl.when(ia == 0)
+            def _():
+                wsecond_copy(ib, first).wait_recv()
+                for direction in range(2):
+                    wfull_copy(direction, ib, first).start()
+
             for direction in range(2):
 
-                @pl.when(kind == 1 + direction)
+                @pl.when(ia == 1 + direction)
                 def _(direction=direction):
-                    wfull_copy(direction, slot, first, second).wait_recv()
-                    whalf_copy(direction, slot, first, second).start()
-
-            @pl.when(kind == 3)
+                    wfull_copy(direction, ib, first).wait_recv()
+                    whalf_copy(direction, ib, first).start()
+
+            @pl.when(ia == 3)
             def _():
                 for direction in range(2):
-                    whalf_copy(direction, slot, first, second).wait_recv()
-
-            @pl.when(second == 1)
-            def _():
-                for direction in range(2):
-                    wfull_copy(direction, ib, first, 0).start()
+                    whalf_copy(direction, ib, first).wait_recv()
 
             wcore_copy(step).start()
-            apply_units(first)
+            apply_units(first, step)
             apply_other(step - 1)
 
+        for ib in (3, 2, 1):
+            wsecond_copy(ib, mine).start()
         for direction in range(2):
-            wfull_copy(direction, 4, mine, 1).start()
-        for direction in range(2):
-            wfull_copy(direction, 0, mine, 0).start()
+            wfull_copy(direction, 0, mine).start()
         wcore_copy(0).start()
-        apply_units(mine)
+        apply_units(mine, 0)
         each(1, 16, take)
         apply_other(15)
 
         def drain_core(step):
             core_copy(step).wait_send()
             wcore_copy(step).wait_send()
+            if rnd == 1:
+                out_copy(0, step).wait()
+                out_copy(0, 16 + step).wait()
 
         def drain_plane(slot):
             for direction in range(2):
-                relay_copy(direction, slot, 0, 0).wait_send()
-                inbox_copy(direction, slot, 0, 0).wait_send()
-                wfull_copy(direction, slot, 0, 0).wait_send()
-                whalf_copy(direction, slot, 0, 0).wait_send()
+                relay_copy(direction, slot, 0).wait_send()
+                inbox_copy(direction, slot, 0).wait_send()
+                wfull_copy(direction, slot, 0).wait_send()
+                whalf_copy(direction, slot, 0).wait_send()
+
+        def drain_second(ib):
+            second_copy(ib, 0).wait_send()
+            wsecond_copy(ib + 1, 0).wait_send()
 
         def drain_z(step):
             zr_copy(step).wait_send()
             zg_copy(step).wait_send()
 
         each(0, 16, drain_core)
-        each(0, 5, drain_plane)
+        each(0, 4, drain_plane)
+        each(0, 3, drain_second)
         each(1, NZ, drain_z)
 
-    one_round(0, table, rotated)
-    one_round(1, rotated, out)
-
-
-STEP = 8
+    one_round(0, (high0, low0))
+    one_round(1, (high1, low1))
 
 
 def last_kernel(assign, pairing, source, out, places):
@@ -498,27 +548,31 @@
 
 def rounds(assignment, pairing, x):
     dma = pltpu.SemaphoreType.DMA
-    chunks, plane, ring = dma((2, 16)), dma((2, 2, 5)), dma((2, NZ))
+    chunks, plane, second, ring = dma((2, 16)), dma((2, 2, 4)), dma((2, 4)), dma((2, NZ))
+    part = pltpu.VMEM((BLOCKS, 2, BLOCK, 128), BF16)
     return pl.pallas_call(
         fused_kernel,
         out_shape=jax.ShapeDtypeStruct(TABLE, F32),
-        in_specs=[SMEM, SMEM, VMEM],
-        out_specs=VMEM,
+        in_specs=[SMEM, SMEM, pl.BlockSpec(memory_space=pl.ANY)],
+        out_specs=pl.BlockSpec(memory_space=pl.ANY),
         scratch_shapes=[
+            pltpu.VMEM((GROUPS, 64, 2 * STEP, 128), F32),
             pltpu.VMEM(TABLE, F32),
-            pltpu.VMEM(TABLE, F32),
+            part, part, part, part,
             pltpu.VMEM((UNITS, 64, 128), F32),
             pltpu.VMEM((2, UNITS // 2, 64, 128), F32),
-            pltpu.VMEM((2, 2, 5, 64, 128), F32),
-            pltpu.VMEM((2, 2, 5, CHUNK, 64, 128), F32),
+            pltpu.VMEM((2, 2, 4, 64, 128), F32),
+            pltpu.VMEM((2, 2, 4, CHUNK, 64, 128), F32),
+            pltpu.VMEM((2, 3, CHUNK, 64, 128), F32),
             pltpu.VMEM((CHUNK, 64, 128), F32),
             pltpu.VMEM((NZ, CHUNK, SLICE, 128), F32),
             pltpu.VMEM((2, NZ, CHUNK, SLICE, 128), F32),
             pltpu.VMEM((CHUNK, SLICE, 128), F32),
             pltpu.VMEM((2, NZ, CHUNK, SLICE, 128), F32),
             pltpu.VMEM((2, UNITS, 64, 128), F32),
-            chunks, chunks, plane, plane, plane, plane, ring, ring, ring, ring,
-            plane, plane, plane, plane, chunks, chunks,
+            dma((GROUPS,)), dma((32,)),
+            chunks, chunks, plane, plane, plane, plane, second, second, ring, ring, ring, ring,
+            plane, plane, plane, plane, second, second, chunks, chunks,
         ],
         compiler_params=PARAMS(collective_id=0, has_side_effects=True),
         name="rounds",
@@ -541,7 +595,7 @@
 
 def on_device(transmission, assignment, pairing):
     rows, _, cols = transmission.shape
-    x = transmission.reshape(rows, 2, cols // 128, 128).transpose(0, 2, 1, 3).reshape(-1, 128)
+    x = transmission.reshape(rows, 2, cols // 128, 128).transpose(0, 2, 1, 3).reshape(rows, -1, 128)
     turned_blocks = rounds(assignment, pairing, x)
     out = unturned(assignment, pairing, turned_blocks)
     out = out.reshape(rows, cols // 128, 2, 128).transpose(0, 2, 1, 3)

time: 134 us -> 121 us (0.903)
  Pallas kernels: 133 us -> 121 us
    pallas_call x1, Pallas kernels: 126 us -> 113 us  [rounds(): pl.pallas_call(fused_kernel, out_shape=jax.ShapeDtypeStruct(TABLE, F32),...]
where the time goes in v4:
time: 121 us
  Pallas kernels  121 us (100%)
    pallas_call x1, Pallas kernels, rounds(): pl.pallas_call(fused_kernel, out_shape=jax.ShapeDtypeStruct(TABLE, F32),...  113 us
    pallas_call x1, Pallas kernels, unturned(): pl.pallas_call(last_kernel, out_shape=jax.ShapeDtypeStruct(shape, F32), g...  7.72 us

profile of v4, /device:TPU:1, one launch (start us, length us, event | category | flops | bytes accessed | tf_op | source)
XLA Modules:
  0.0 120.7 jit_solution(69503029950745339)
XLA Ops:
  0.0 113.0 %rounds.1.source = f32[256,32,128]{2,1,0:T(8,128)} custom-call(s32[256]{0:T(256)} %assign.3, s32[2,64]{1,0:T(2,128)} %pairing.3, f32[64,128,128]{2,1,0:T(8,128)} %bitcast.10), custom_call_target="tpu_custom_call" | custom-call | tf_op jit(solution)/shard_map/rounds/pallas_call | solution.py:553
  113.0 7.7 %unturn.1 = f32[64,128,128]{2,1,0:T(8,128)} custom-call(s32[256]{0:T(256)} %assign.3, s32[2,64]{1,0:T(2,128)} %pairing.3, f32[256,32,128]{2,1,0:T(8,128)} %rounds.1.source), custom_call_target="tpu_custom_call" | custom-call | tf_op jit(solution)/shard_map/unturn/pallas_call | solution.py:584

commit v5 on v4

--- a/solution.py
+++ b/solution.py
@@ -19,7 +19,8 @@
 NX, NY, NZ = 4, 4, 8
 NXY = NX * NY
 CHUNK = UNITS // 2 // NXY
-SLICE = 64 // NZ
+DEPTH = 3 * 64
+SLICE = DEPTH // NZ
 STEP = 8
 GROUPS = BLOCKS // 4 // STEP
 PARAMS = functools.partial(pltpu.CompilerParams, vmem_limit_bytes=60 * 1024 * 1024)
@@ -39,6 +40,11 @@
 
 def turn_of(slot):
     return jnp.where(slot == 1, -1, jnp.where(slot == 2, 1, 0))
+
+
+def home_of(pairing, d, slot):
+    home = lax.rem(d + turn_of(slot) + UNITS, UNITS)
+    return home, position(pairing[0, home], slot)
 
 
 def pair_places(assign, pairing, rnd, d, h):
@@ -47,9 +53,17 @@
         return [assign[d * SLOTS + slot] for slot in slots]
     places = []
     for slot in slots:
-        home = lax.rem(d + turn_of(slot) + UNITS, UNITS)
-        places.append(home * SLOTS + position(pairing[0, home], slot))
+        home, place = home_of(pairing, d, slot)
+        places.append(home * SLOTS + place)
     return places
+
+
+def pair_around(assign, pairing, home, place):
+    pick = pairing[0, home]
+    in_first = place < 2
+    first = jnp.where(in_first, 0, jnp.where(pick == 0, 2, 1))
+    second = jnp.where(in_first, 1 + pick, jnp.where(pick == 2, 2, 3))
+    return assign[home * SLOTS + first], assign[home * SLOTS + second]
 
 
 def lanes_of(shape):
@@ -110,6 +124,15 @@
     lhs = jnp.concatenate([high[pair], low[pair]], axis=1)
     rhs = jnp.concatenate([high, high], axis=1)
     return nt_dot(lhs, rhs) + nt_dot(high[pair], low)
+
+
+def cross_top(tables, left, right):
+    lhigh = jnp.concatenate([tables[0][k, 0] for k in left], axis=0)
+    llow = jnp.concatenate([tables[1][k, 0] for k in left], axis=0)
+    high, low = parts_of(tables[0], *right), parts_of(tables[1], *right)
+    lhs = jnp.concatenate([lhigh, llow], axis=1)
+    rhs = jnp.concatenate([high, high], axis=1)
+    return nt_dot(lhs, rhs) + nt_dot(lhigh, low)
 
 
 def applied(top, tables, a, b):
@@ -178,6 +201,29 @@
     return [z * jnp.sqrt(ROWS / s) for z, s in zip(lower, scales)]
 
 
+def triple(left, middle, right):
+    return fdot(fdot(left, full(middle)), full(right))
+
+
+def sided(value, side, wanted, axis, back):
+    moved = pltpu.roll(value, back, axis)
+    return jnp.where(jnp.full(value.shape, side, jnp.int32) == wanted, value, moved)
+
+
+def next_gram(cross, gram_u, gram_v, side_u, side_v):
+    shape = cross.shape
+    lane, row = lanes_of(shape), rows_of(shape)
+    upper = sided(sided(cross, side_u, 0, 0, 32), side_v, 1, 1, 32)
+    corner_u = sided(sided(gram_u, side_u, 0, 0, 32), side_u, 0, 1, 96)
+    corner_v = sided(sided(gram_v, side_v, 1, 0, 32), side_v, 1, 1, 32)
+    flipped = jnp.concatenate([upper, upper], axis=0).T
+    lower = jnp.where(lane < 64, flipped[:64], -flipped[64:])
+    early = lax.rem(lane, 64) < 32
+    return jnp.where(
+        row < 32, jnp.where(early, corner_u, upper), jnp.where(early, lower, corner_v)
+    )
+
+
 def order_in(i):
     return lax.rem(2 + 3 * i + 3 * (i * (i - 1) // 2), 4)
 
@@ -188,10 +234,11 @@
 
 def fused_kernel(
     assign, pairing, x_in, out, x_held, results, high0, low0, high1, low1, packed, from_core, relay,
-    inbox, second_in, total, slices, from_z, mine_z, gathered, weights, x_sem, out_sem,
+    inbox, second_in, total, slices, from_z, mine_z, gathered, weights, near, roots_near, grams_near,
+    near_in, x_sem, out_sem,
     core_send, core_recv, relay_send, relay_recv, inbox_send, inbox_recv, second_send, second_recv, zr_send,
     zr_recv, zg_send, zg_recv, wfull_send, wfull_recv, whalf_send, whalf_recv, wsecond_send,
-    wsecond_recv, wcore_send, wcore_recv,
+    wsecond_recv, wcore_send, wcore_recv, near_send, near_recv,
 ):
     blk, row = lax.axis_index("blk"), lax.axis_index("row")
     y_lo, z, x = blk // (NZ * NX), lax.rem(blk // NX, NZ), lax.rem(blk, NX)
@@ -214,6 +261,11 @@
 
     partner = device(y, z, x, 1 - core)
 
+    def owner(move):
+        chunk = lax.rem(core * NXY + p * 4 + q + move, 2 * NXY)
+        cc, pp, qq = chunk // NXY, lax.rem(chunk // 4, 4), lax.rem(chunk, 4)
+        return device(qq + cc * (pp - qq), z, pp + cc * (qq - pp), cc)
+
     def ring_device(step):
         return device(y, lax.rem(z + step, NZ), x, core)
 
@@ -247,6 +299,8 @@
         greet(across(distance))
     for step in range(1, NZ):
         greet(ring_device(step))
+    greet(owner(1))
+    greet(owner(2 * NXY - 1))
 
     def x_copy(group):
         return pltpu.make_async_copy(
@@ -264,44 +318,52 @@
 
     each(0, GROUPS, lambda group: x_copy(group).start())
     each(0, GROUPS, load_group)
-    pl.semaphore_wait(barrier, 6 + NZ - 1)
-
-    def one_round(rnd, source):
+    pl.semaphore_wait(barrier, 8 + NZ - 1)
+
+    def reduced():
+        source = (high0, low0)
+
         def core_copy(step):
             place = other_chunk(order_in(step // 4), order_in(lax.rem(step, 4)))
             return remote(
                 packed.at[pl.ds((1 - core) * half + place, CHUNK)],
-                from_core.at[rnd, pl.ds(place, CHUNK)],
-                core_send.at[rnd, step], core_recv.at[rnd, step], partner,
+                from_core.at[pl.ds(place, CHUNK)],
+                core_send.at[step], core_recv.at[step], partner,
             )
 
         def relay_copy(direction, slot, place):
             return remote(
-                from_core.at[rnd, place + direction], relay.at[rnd, direction, slot],
-                relay_send.at[rnd, direction, slot], relay_recv.at[rnd, direction, slot],
+                from_core.at[place + direction], relay.at[direction, slot],
+                relay_send.at[direction, slot], relay_recv.at[direction, slot],
                 beside(direction),
             )
 
         def inbox_copy(direction, slot, place):
             return remote(
-                from_core.at[rnd, pl.ds(place, CHUNK)], inbox.at[rnd, direction, slot],
-                inbox_send.at[rnd, direction, slot], inbox_recv.at[rnd, direction, slot],
+                from_core.at[pl.ds(place, CHUNK)], inbox.at[direction, slot],
+                inbox_send.at[direction, slot], inbox_recv.at[direction, slot],
                 beside(direction),
             )
 
         def second_copy(ib, place):
             return remote(
-                from_core.at[rnd, pl.ds(place, CHUNK)], second_in.at[rnd, ib],
-                second_send.at[rnd, ib], second_recv.at[rnd, ib], across(order_in(ib)),
+                from_core.at[pl.ds(place, CHUNK)], second_in.at[ib],
+                second_send.at[ib], second_recv.at[ib], across(order_in(ib)),
             )
 
         def gram_units(first):
             for u in range(CHUNK):
+                d = first + u
                 tops = []
                 for h in range(2):
-                    a, b = pair_places(assign, pairing, rnd, first + u, h)
+                    a, b = pair_places(assign, pairing, 0, d, h)
                     tops.append(gram_top(source, a, b, h == 1))
-                packed[first + u] = pack(*tops)
+                    slots = slot_at(pairing[1, d], h)
+                    around = [
+                        pair_around(assign, pairing, *home_of(pairing, d, slot)) for slot in slots
+                    ]
+                    packed[d, pl.ds(64 + 64 * h, 64)] = cross_top(source, *around)
+                packed[d, pl.ds(0, 64)] = pack(*tops)
 
         def compute(step):
             da, db = order_in(step // 4), order_in(lax.rem(step, 4))
@@ -312,14 +374,14 @@
         def inbox_sum(slot):
             for direction in range(2):
                 inbox_copy(direction, slot, 0).wait_recv()
-            return inbox[rnd, 0, slot] + inbox[rnd, 1, slot]
+            return inbox[0, slot] + inbox[1, slot]
 
         def ship(step):
             ia, ib = step // 4, lax.rem(step, 4)
             place = my_chunk(order_in(ia), order_in(ib))
             chunk = pl.ds(place, CHUNK)
             core_copy(step).wait_recv()
-            from_core[rnd, chunk] += packed[pl.ds(core * half + place, CHUNK)]
+            from_core[chunk] += packed[pl.ds(core * half + place, CHUNK)]
 
             @pl.when(ia == 0)
             def _():
@@ -331,12 +393,12 @@
                 @pl.when(ia == 1 + direction)
                 def _(direction=direction):
                     relay_copy(direction, ib, place).wait_recv()
-                    from_core[rnd, place + direction] += relay[rnd, direction, ib]
+                    from_core[place + direction] += relay[direction, ib]
                     inbox_copy(direction, ib, place).start()
 
             @pl.when(ia == 3)
             def _():
-                from_core[rnd, chunk] += inbox_sum(ib)
+                from_core[chunk] += inbox_sum(ib)
                 second_copy(ib, place).start()
 
         def advance(step):
@@ -348,26 +410,26 @@
         core_copy(15).wait_recv()
         place = my_chunk(0, 0)
         total[...] = (
-            from_core[rnd, pl.ds(place, CHUNK)]
+            from_core[pl.ds(place, CHUNK)]
             + packed[pl.ds(core * half + place, CHUNK)]
             + inbox_sum(3)
         )
         for ib in range(3):
             second_copy(ib, 0).wait_recv()
-            total[...] += second_in[rnd, ib]
+            total[...] += second_in[ib]
 
         for k in range(NZ):
             slices[k] = total[:, k * SLICE : (k + 1) * SLICE, :]
 
         def zr_copy(step):
             return remote(
-                slices.at[lax.rem(z + step, NZ)], from_z.at[rnd, step],
-                zr_send.at[rnd, step], zr_recv.at[rnd, step], ring_device(step),
+                slices.at[lax.rem(z + step, NZ)], from_z.at[step],
+                zr_send.at[step], zr_recv.at[step], ring_device(step),
             )
 
         def zg_copy(step):
             return remote(
-                mine_z, gathered.at[rnd, z], zg_send.at[rnd, step], zg_recv.at[rnd, step],
+                mine_z, gathered.at[z], zg_send.at[step], zg_recv.at[step],
                 ring_device(step),
             )
 
@@ -377,21 +439,39 @@
         acc = slices[z]
         for step in reversed(far_first):
             zr_copy(step).wait_recv()
-            acc = acc + from_z[rnd, step]
+            acc = acc + from_z[step]
         mine_z[...] = acc
         for step in far_first:
             zg_copy(step).start()
-        gathered[rnd, z] = acc
+        gathered[z] = acc
         for step in reversed(far_first):
             zg_copy(step).wait_recv()
 
-        tops = []
-        for u in range(CHUNK):
-            tops.extend(unpack(gathered[rnd, :, u].reshape(64, 128)))
-        roots = inverse_roots(tops)
-        mine = core * half + place
-        for u in range(CHUNK):
-            weights[rnd, mine + u] = pack(roots[2 * u], pltpu.roll(roots[2 * u + 1], 64, 1))
+        def drain_core(step):
+            core_copy(step).wait_send()
+
+        def drain_plane(slot):
+            for direction in range(2):
+                relay_copy(direction, slot, 0).wait_send()
+                inbox_copy(direction, slot, 0).wait_send()
+
+        def drain_second(ib):
+            second_copy(ib, 0).wait_send()
+
+        def drain_z(step):
+            zr_copy(step).wait_send()
+            zg_copy(step).wait_send()
+
+        def drain():
+            each(0, 16, drain_core)
+            each(0, 4, drain_plane)
+            each(0, 3, drain_second)
+            each(1, NZ, drain_z)
+
+        return drain
+
+    def handing(rnd, source):
+        mine = core * half + my_chunk(0, 0)
 
         def wfull_copy(direction, slot, first):
             part = weights.at[rnd, pl.ds(first, CHUNK)]
@@ -459,12 +539,12 @@
                 for direction in range(2):
                     wfull_copy(direction, ib, first).start()
 
-            for direction in range(2):
-
-                @pl.when(ia == 1 + direction)
-                def _(direction=direction):
-                    wfull_copy(direction, ib, first).wait_recv()
-                    whalf_copy(direction, ib, first).start()
+            @pl.when(ia == 1)
+            def _():
+                for direction in range(2):
+                    whole = my_units(step + 4 * direction)
+                    wfull_copy(direction, ib, whole).wait_recv()
+                    whalf_copy(direction, ib, whole).start()
 
             @pl.when(ia == 3)
             def _():
@@ -475,17 +555,19 @@
             apply_units(first, step)
             apply_other(step - 1)
 
-        for ib in (3, 2, 1):
-            wsecond_copy(ib, mine).start()
-        for direction in range(2):
-            wfull_copy(direction, 0, mine).start()
-        wcore_copy(0).start()
-        apply_units(mine, 0)
-        each(1, 16, take)
-        apply_other(15)
+        def begin():
+            for ib in (3, 2, 1):
+                wsecond_copy(ib, mine).start()
+            for direction in range(2):
+                wfull_copy(direction, 0, mine).start()
+            wcore_copy(0).start()
+
+        def finish():
+            apply_units(mine, 0)
+            each(1, 16, take)
+            apply_other(15)
 
         def drain_core(step):
-            core_copy(step).wait_send()
             wcore_copy(step).wait_send()
             if rnd == 1:
                 out_copy(0, step).wait()
@@ -493,26 +575,79 @@
 
         def drain_plane(slot):
             for direction in range(2):
-                relay_copy(direction, slot, 0).wait_send()
-                inbox_copy(direction, slot, 0).wait_send()
                 wfull_copy(direction, slot, 0).wait_send()
                 whalf_copy(direction, slot, 0).wait_send()
 
-        def drain_second(ib):
-            second_copy(ib, 0).wait_send()
-            wsecond_copy(ib + 1, 0).wait_send()
-
-        def drain_z(step):
-            zr_copy(step).wait_send()
-            zg_copy(step).wait_send()
-
-        each(0, 16, drain_core)
-        each(0, 4, drain_plane)
-        each(0, 3, drain_second)
-        each(1, NZ, drain_z)
-
-    one_round(0, (high0, low0))
-    one_round(1, (high1, low1))
+        def drain():
+            each(0, 16, drain_core)
+            each(0, 4, drain_plane)
+            each(1, 4, lambda ib: wsecond_copy(ib, 0).wait_send())
+
+        return begin, finish, drain
+
+    drain_reduced = reduced()
+    begin0, finish0, drain0 = handing(0, (high0, low0))
+    begin1, finish1, drain1 = handing(1, (high1, low1))
+    mine = core * half + my_chunk(0, 0)
+
+    units = [gathered[:, u].reshape(DEPTH, 128) for u in range(CHUNK)]
+    tops = []
+    for unit in units:
+        tops.extend(unpack(unit[:64]))
+    roots = inverse_roots(tops)
+
+    def packed_pair(values, u):
+        return pack(values[2 * u], pltpu.roll(values[2 * u + 1], 64, 1))
+
+    def near_copy(which):
+        return remote(
+            near.at[1 - which], near_in.at[which], near_send.at[which], near_recv.at[which],
+            owner(1 if which == 0 else 2 * NXY - 1),
+        )
+
+    inner = [triple(w, g, w) for w, g in zip(roots, tops)]
+    for u in range(CHUNK):
+        near[u, 0] = packed_pair(roots, u)
+        near[u, 1] = packed_pair(inner, u)
+    for which in range(2):
+        near_copy(which).start()
+    for u in range(CHUNK):
+        weights[0, mine + u] = near[u, 0]
+        for h in range(2):
+            roots_near[2 + 2 * u + h] = roots[2 * u + h]
+            grams_near[2 + 2 * u + h] = inner[2 * u + h]
+    begin0()
+    for which in range(2):
+        near_copy(which).wait_recv()
+        for kind, table in enumerate((roots_near, grams_near)):
+            for h, top in enumerate(unpack(near_in[which, kind])):
+                table[6 * which + h] = top
+
+    tops = []
+    for u in range(CHUNK):
+        for h in range(2):
+            d = mine + u
+            found = []
+            for slot in slot_at(pairing[1, d], h):
+                _, place = home_of(pairing, d, slot)
+                index = 2 * (1 + u + turn_of(slot)) + place // 2
+                found.append((index, lax.rem(place, 2)))
+            (left, side_u), (right, side_v) = found
+            cross = triple(
+                roots_near[left], units[u][64 + 64 * h : 128 + 64 * h], roots_near[right]
+            )
+            tops.append(next_gram(cross, grams_near[left], grams_near[right], side_u, side_v))
+    roots = inverse_roots(tops)
+    for u in range(CHUNK):
+        weights[1, mine + u] = packed_pair(roots, u)
+    begin1()
+    finish0()
+    finish1()
+    drain_reduced()
+    drain0()
+    drain1()
+    for which in range(2):
+        near_copy(which).wait_send()
 
 
 def last_kernel(assign, pairing, source, out, places):
@@ -548,7 +683,7 @@
 
 def rounds(assignment, pairing, x):
     dma = pltpu.SemaphoreType.DMA
-    chunks, plane, second, ring = dma((2, 16)), dma((2, 2, 4)), dma((2, 4)), dma((2, NZ))
+    chunks, plane, second, ring = dma((2, 16)), dma((2, 2, 4)), dma((2, 4)), dma((NZ,))
     part = pltpu.VMEM((BLOCKS, 2, BLOCK, 128), BF16)
     return pl.pallas_call(
         fused_kernel,
@@ -559,20 +694,25 @@
             pltpu.VMEM((GROUPS, 64, 2 * STEP, 128), F32),
             pltpu.VMEM(TABLE, F32),
             part, part, part, part,
-            pltpu.VMEM((UNITS, 64, 128), F32),
-            pltpu.VMEM((2, UNITS // 2, 64, 128), F32),
-            pltpu.VMEM((2, 2, 4, 64, 128), F32),
-            pltpu.VMEM((2, 2, 4, CHUNK, 64, 128), F32),
-            pltpu.VMEM((2, 3, CHUNK, 64, 128), F32),
-            pltpu.VMEM((CHUNK, 64, 128), F32),
+            pltpu.VMEM((UNITS, DEPTH, 128), F32),
+            pltpu.VMEM((UNITS // 2, DEPTH, 128), F32),
+            pltpu.VMEM((2, 4, DEPTH, 128), F32),
+            pltpu.VMEM((2, 4, CHUNK, DEPTH, 128), F32),
+            pltpu.VMEM((3, CHUNK, DEPTH, 128), F32),
+            pltpu.VMEM((CHUNK, DEPTH, 128), F32),
             pltpu.VMEM((NZ, CHUNK, SLICE, 128), F32),
-            pltpu.VMEM((2, NZ, CHUNK, SLICE, 128), F32),
+            pltpu.VMEM((NZ, CHUNK, SLICE, 128), F32),
             pltpu.VMEM((CHUNK, SLICE, 128), F32),
-            pltpu.VMEM((2, NZ, CHUNK, SLICE, 128), F32),
+            pltpu.VMEM((NZ, CHUNK, SLICE, 128), F32),
             pltpu.VMEM((2, UNITS, 64, 128), F32),
+            pltpu.VMEM((2, 2, 64, 128), F32),
+            pltpu.VMEM((8, 64, 128), F32),
+            pltpu.VMEM((8, 64, 128), F32),
+            pltpu.VMEM((2, 2, 64, 128), F32),
             dma((GROUPS,)), dma((32,)),
-            chunks, chunks, plane, plane, plane, plane, second, second, ring, ring, ring, ring,
-            plane, plane, plane, plane, second, second, chunks, chunks,
+            dma((16,)), dma((16,)), dma((2, 4)), dma((2, 4)), dma((2, 4)), dma((2, 4)),
+            dma((4,)), dma((4,)), ring, ring, ring, ring,
+            plane, plane, plane, plane, second, second, chunks, chunks, dma((2,)), dma((2,)),
         ],
         compiler_params=PARAMS(collective_id=0, has_side_effects=True),
         name="rounds",

time: 121 us -> 102 us (0.84)
  Pallas kernels: 121 us -> 102 us
    pallas_call x1, Pallas kernels: 113 us -> 94 us  [rounds(): pl.pallas_call(fused_kernel, out_shape=jax.ShapeDtypeStruct(TABLE, F32),...]
where the time goes in v5:
time: 102 us
  Pallas kernels  102 us (100%)
    pallas_call x1, Pallas kernels, rounds(): pl.pallas_call(fused_kernel, out_shape=jax.ShapeDtypeStruct(TABLE, F32),...  94 us
    pallas_call x1, Pallas kernels, unturned(): pl.pallas_call(last_kernel, out_shape=jax.ShapeDtypeStruct(shape, F32), g...  7.72 us

profile of v5, /device:TPU:1, one launch (start us, length us, event | category | flops | bytes accessed | tf_op | source)
XLA Modules:
  0.0 101.8 jit_solution(2759972857024189879)
XLA Ops:
  0.0 94.0 %rounds.1.source = f32[256,32,128]{2,1,0:T(8,128)} custom-call(s32[256]{0:T(256)} %assign.3, s32[2,64]{1,0:T(2,128)} %pairing.3, f32[64,128,128]{2,1,0:T(8,128)} %bitcast.10), custom_call_target="tpu_custom_call" | custom-call | tf_op jit(solution)/shard_map/rounds/pallas_call | solution.py:688
  94.0 7.7 %unturn.1 = f32[64,128,128]{2,1,0:T(8,128)} custom-call(s32[256]{0:T(256)} %assign.3, s32[2,64]{1,0:T(2,128)} %pairing.3, f32[256,32,128]{2,1,0:T(8,128)} %rounds.1.source), custom_call_target="tpu_custom_call" | custom-call | tf_op jit(solution)/shard_map/unturn/pallas_call | solution.py:724

commit v6 on v5

--- a/solution.py
+++ b/solution.py
@@ -20,7 +20,7 @@
 NXY = NX * NY
 CHUNK = UNITS // 2 // NXY
 DEPTH = 3 * 64
-SLICE = DEPTH // NZ
+SLICES = (64 // NZ, 128 // NZ)
 STEP = 8
 GROUPS = BLOCKS // 4 // STEP
 PARAMS = functools.partial(pltpu.CompilerParams, vmem_limit_bytes=60 * 1024 * 1024)
@@ -234,7 +234,8 @@
 
 def fused_kernel(
     assign, pairing, x_in, out, x_held, results, high0, low0, high1, low1, packed, from_core, relay,
-    inbox, second_in, total, slices, from_z, mine_z, gathered, weights, near, roots_near, grams_near,
+    inbox, second_in, total, slices_0, from_z_0, mine_z_0, gathered_0, slices_1, from_z_1, mine_z_1,
+    gathered_1, weights, near, roots_near, grams_near,
     near_in, x_sem, out_sem,
     core_send, core_recv, relay_send, relay_recv, inbox_send, inbox_recv, second_send, second_recv, zr_send,
     zr_recv, zg_send, zg_recv, wfull_send, wfull_recv, whalf_send, whalf_recv, wsecond_send,
@@ -319,6 +320,9 @@
     each(0, GROUPS, lambda group: x_copy(group).start())
     each(0, GROUPS, load_group)
     pl.semaphore_wait(barrier, 8 + NZ - 1)
+
+    slices, from_z = (slices_0, slices_1), (from_z_0, from_z_1)
+    mine_z, gathered = (mine_z_0, mine_z_1), (gathered_0, gathered_1)
 
     def reduced():
         source = (high0, low0)
@@ -418,34 +422,41 @@
             second_copy(ib, 0).wait_recv()
             total[...] += second_in[ib]
 
-        for k in range(NZ):
-            slices[k] = total[:, k * SLICE : (k + 1) * SLICE, :]
-
-        def zr_copy(step):
-            return remote(
-                slices.at[lax.rem(z + step, NZ)], from_z.at[step],
-                zr_send.at[step], zr_recv.at[step], ring_device(step),
-            )
-
-        def zg_copy(step):
-            return remote(
-                mine_z, gathered.at[z], zg_send.at[step], zg_recv.at[step],
+        for part, size in enumerate(SLICES):
+            for k in range(NZ):
+                begin = 64 * part + k * size
+                slices[part][k] = total[:, begin : begin + size, :]
+
+        def zr_copy(part, step):
+            return remote(
+                slices[part].at[lax.rem(z + step, NZ)], from_z[part].at[step],
+                zr_send.at[part, step], zr_recv.at[part, step], ring_device(step),
+            )
+
+        def zg_copy(part, step):
+            return remote(
+                mine_z[part], gathered[part].at[z], zg_send.at[part, step], zg_recv.at[part, step],
                 ring_device(step),
             )
 
         far_first = (4, 3, 5, 2, 6, 1, 7)
-        for step in far_first:
-            zr_copy(step).start()
-        acc = slices[z]
-        for step in reversed(far_first):
-            zr_copy(step).wait_recv()
-            acc = acc + from_z[step]
-        mine_z[...] = acc
-        for step in far_first:
-            zg_copy(step).start()
-        gathered[z] = acc
-        for step in reversed(far_first):
-            zg_copy(step).wait_recv()
+        for part in range(2):
+            for step in far_first:
+                zr_copy(part, step).start()
+        for part in range(2):
+            acc = slices[part][z]
+            for step in reversed(far_first):
+                zr_copy(part, step).wait_recv()
+                acc = acc + from_z[part][step]
+            mine_z[part][...] = acc
+            for step in far_first:
+                zg_copy(part, step).start()
+            gathered[part][z] = acc
+
+        def units_of(part):
+            for step in reversed(far_first):
+                zg_copy(part, step).wait_recv()
+            return [gathered[part][:, u].reshape(NZ * SLICES[part], 128) for u in range(CHUNK)]
 
         def drain_core(step):
             core_copy(step).wait_send()
@@ -459,8 +470,9 @@
             second_copy(ib, 0).wait_send()
 
         def drain_z(step):
-            zr_copy(step).wait_send()
-            zg_copy(step).wait_send()
+            for part in range(2):
+                zr_copy(part, step).wait_send()
+                zg_copy(part, step).wait_send()
 
         def drain():
             each(0, 16, drain_core)
@@ -468,7 +480,7 @@
             each(0, 3, drain_second)
             each(1, NZ, drain_z)
 
-        return drain
+        return units_of, drain
 
     def handing(rnd, source):
         mine = core * half + my_chunk(0, 0)
@@ -525,11 +537,7 @@
             if rnd == 1:
                 out_copy(first, which).start()
 
-        def apply_other(step):
-            wcore_copy(step).wait_recv()
-            apply_units(other_units(step), 16 + step)
-
-        def take(step):
+        def forward(step):
             ia, ib = step // 4, lax.rem(step, 4)
             first = my_units(step)
 
@@ -552,8 +560,13 @@
                     whalf_copy(direction, ib, first).wait_recv()
 
             wcore_copy(step).start()
-            apply_units(first, step)
-            apply_other(step - 1)
+
+        def use(step):
+            apply_units(my_units(step), step)
+
+        def use_other(step):
+            wcore_copy(step).wait_recv()
+            apply_units(other_units(step), 16 + step)
 
         def begin():
             for ib in (3, 2, 1):
@@ -562,11 +575,6 @@
                 wfull_copy(direction, 0, mine).start()
             wcore_copy(0).start()
 
-        def finish():
-            apply_units(mine, 0)
-            each(1, 16, take)
-            apply_other(15)
-
         def drain_core(step):
             wcore_copy(step).wait_send()
             if rnd == 1:
@@ -583,17 +591,16 @@
             each(0, 4, drain_plane)
             each(1, 4, lambda ib: wsecond_copy(ib, 0).wait_send())
 
-        return begin, finish, drain
-
-    drain_reduced = reduced()
-    begin0, finish0, drain0 = handing(0, (high0, low0))
-    begin1, finish1, drain1 = handing(1, (high1, low1))
+        return begin, forward, use, use_other, drain
+
+    units_of, drain_reduced = reduced()
+    begin0, forward0, use0, use_other0, drain0 = handing(0, (high0, low0))
+    begin1, forward1, use1, use_other1, drain1 = handing(1, (high1, low1))
     mine = core * half + my_chunk(0, 0)
 
-    units = [gathered[:, u].reshape(DEPTH, 128) for u in range(CHUNK)]
     tops = []
-    for unit in units:
-        tops.extend(unpack(unit[:64]))
+    for unit in units_of(0):
+        tops.extend(unpack(unit))
     roots = inverse_roots(tops)
 
     def packed_pair(values, u):
@@ -617,6 +624,15 @@
             roots_near[2 + 2 * u + h] = roots[2 * u + h]
             grams_near[2 + 2 * u + h] = inner[2 * u + h]
     begin0()
+    use0(0)
+
+    def take0(step):
+        forward0(step)
+        use0(step)
+        use_other0(step - 1)
+
+    each(1, 4, take0)
+    crosses = units_of(1)
     for which in range(2):
         near_copy(which).wait_recv()
         for kind, table in enumerate((roots_near, grams_near)):
@@ -634,15 +650,32 @@
                 found.append((index, lax.rem(place, 2)))
             (left, side_u), (right, side_v) = found
             cross = triple(
-                roots_near[left], units[u][64 + 64 * h : 128 + 64 * h], roots_near[right]
+                roots_near[left], crosses[u][64 * h : 64 * h + 64], roots_near[right]
             )
             tops.append(next_gram(cross, grams_near[left], grams_near[right], side_u, side_v))
     roots = inverse_roots(tops)
     for u in range(CHUNK):
         weights[1, mine + u] = packed_pair(roots, u)
     begin1()
-    finish0()
-    finish1()
+    each(4, 12, take0)
+    each(1, 4, forward1)
+    each(12, 16, take0)
+    use_other0(15)
+    use1(0)
+
+    def take1(step):
+        use1(step)
+        use_other1(step - 1)
+
+    def forward_and_take1(step):
+        forward1(step)
+        take1(step)
+
+    each(1, 4, take1)
+    each(4, 8, forward1)
+    each(4, 8, take1)
+    each(8, 16, forward_and_take1)
+    use_other1(15)
     drain_reduced()
     drain0()
     drain1()
@@ -683,7 +716,7 @@
 
 def rounds(assignment, pairing, x):
     dma = pltpu.SemaphoreType.DMA
-    chunks, plane, second, ring = dma((2, 16)), dma((2, 2, 4)), dma((2, 4)), dma((NZ,))
+    chunks, plane, second, ring = dma((2, 16)), dma((2, 2, 4)), dma((2, 4)), dma((2, NZ))
     part = pltpu.VMEM((BLOCKS, 2, BLOCK, 128), BF16)
     return pl.pallas_call(
         fused_kernel,
@@ -700,10 +733,14 @@
             pltpu.VMEM((2, 4, CHUNK, DEPTH, 128), F32),
             pltpu.VMEM((3, CHUNK, DEPTH, 128), F32),
             pltpu.VMEM((CHUNK, DEPTH, 128), F32),
-            pltpu.VMEM((NZ, CHUNK, SLICE, 128), F32),
-            pltpu.VMEM((NZ, CHUNK, SLICE, 128), F32),
-            pltpu.VMEM((CHUNK, SLICE, 128), F32),
-            pltpu.VMEM((NZ, CHUNK, SLICE, 128), F32),
+            pltpu.VMEM((NZ, CHUNK, SLICES[0], 128), F32),
+            pltpu.VMEM((NZ, CHUNK, SLICES[0], 128), F32),
+            pltpu.VMEM((CHUNK, SLICES[0], 128), F32),
+            pltpu.VMEM((NZ, CHUNK, SLICES[0], 128), F32),
+            pltpu.VMEM((NZ, CHUNK, SLICES[1], 128), F32),
+            pltpu.VMEM((NZ, CHUNK, SLICES[1], 128), F32),
+            pltpu.VMEM((CHUNK, SLICES[1], 128), F32),
+            pltpu.VMEM((NZ, CHUNK, SLICES[1], 128), F32),
             pltpu.VMEM((2, UNITS, 64, 128), F32),
             pltpu.VMEM((2, 2, 64, 128), F32),
             pltpu.VMEM((8, 64, 128), F32),

time: 102 us -> 97.7 us (0.958)
  Pallas kernels: 102 us -> 97.6 us
    pallas_call x1, Pallas kernels: 94 us -> 89.9 us  [rounds(): pl.pallas_call(fused_kernel, out_shape=jax.ShapeDtypeStruct(TABLE, F32),...]
where the time goes in v6:
time: 97.7 us; the launch traced here: 97.6 us
  Pallas kernels  97.6 us (100%)
    pallas_call x1, Pallas kernels, rounds(): pl.pallas_call(fused_kernel, out_shape=jax.ShapeDtypeStruct(TABLE, F32),...  89.9 us
    pallas_call x1, Pallas kernels, unturned(): pl.pallas_call(last_kernel, out_shape=jax.ShapeDtypeStruct(shape, F32), g...  7.72 us

profile of v6, /device:TPU:1, one launch (start us, length us, event | category | flops | bytes accessed | tf_op | source)
XLA Modules:
  0.0 97.6 jit_solution(8956670788679443017)
XLA Ops:
  0.0 89.9 %rounds.1.source = f32[256,32,128]{2,1,0:T(8,128)} custom-call(s32[256]{0:T(256)} %assign.3, s32[2,64]{1,0:T(2,128)} %pairing.3, f32[64,128,128]{2,1,0:T(8,128)} %bitcast.10), custom_call_target="tpu_custom_call" | custom-call | tf_op jit(solution)/shard_map/rounds/pallas_call | solution.py:721
  89.9 7.7 %unturn.1 = f32[64,128,128]{2,1,0:T(8,128)} custom-call(s32[256]{0:T(256)} %assign.3, s32[2,64]{1,0:T(2,128)} %pairing.3, f32[256,32,128]{2,1,0:T(8,128)} %rounds.1.source), custom_call_target="tpu_custom_call" | custom-call | tf_op jit(solution)/shard_map/unturn/pallas_call | solution.py:761

commit v7 on v6

--- a/solution.py
+++ b/solution.py
@@ -19,7 +19,7 @@
 NX, NY, NZ = 4, 4, 8
 NXY = NX * NY
 CHUNK = UNITS // 2 // NXY
-DEPTH = 3 * 64
+DEPTHS = (64, 128)
 SLICES = (64 // NZ, 128 // NZ)
 STEP = 8
 GROUPS = BLOCKS // 4 // STEP
@@ -233,9 +233,10 @@
 
 
 def fused_kernel(
-    assign, pairing, x_in, out, x_held, results, high0, low0, high1, low1, packed, from_core, relay,
-    inbox, second_in, total, slices_0, from_z_0, mine_z_0, gathered_0, slices_1, from_z_1, mine_z_1,
-    gathered_1, weights, near, roots_near, grams_near,
+    assign, pairing, x_in, out, x_held, results, high0, low0, high1, low1,
+    packed_0, from_core_0, relay_0, inbox_0, second_in_0, total_0, slices_0, from_z_0, mine_z_0, gathered_0,
+    packed_1, from_core_1, relay_1, inbox_1, second_in_1, total_1, slices_1, from_z_1, mine_z_1, gathered_1,
+    weights, near, roots_near, grams_near,
     near_in, x_sem, out_sem,
     core_send, core_recv, relay_send, relay_recv, inbox_send, inbox_recv, second_send, second_recv, zr_send,
     zr_recv, zg_send, zg_recv, wfull_send, wfull_recv, whalf_send, whalf_recv, wsecond_send,
@@ -321,38 +322,41 @@
     each(0, GROUPS, load_group)
     pl.semaphore_wait(barrier, 8 + NZ - 1)
 
+    packed, from_core = (packed_0, packed_1), (from_core_0, from_core_1)
+    relay, inbox = (relay_0, relay_1), (inbox_0, inbox_1)
+    second_in, total = (second_in_0, second_in_1), (total_0, total_1)
     slices, from_z = (slices_0, slices_1), (from_z_0, from_z_1)
     mine_z, gathered = (mine_z_0, mine_z_1), (gathered_0, gathered_1)
 
-    def reduced():
+    def reduction(part):
         source = (high0, low0)
 
         def core_copy(step):
             place = other_chunk(order_in(step // 4), order_in(lax.rem(step, 4)))
             return remote(
-                packed.at[pl.ds((1 - core) * half + place, CHUNK)],
-                from_core.at[pl.ds(place, CHUNK)],
-                core_send.at[step], core_recv.at[step], partner,
+                packed[part].at[pl.ds((1 - core) * half + place, CHUNK)],
+                from_core[part].at[pl.ds(place, CHUNK)],
+                core_send.at[part, step], core_recv.at[part, step], partner,
             )
 
         def relay_copy(direction, slot, place):
             return remote(
-                from_core.at[place + direction], relay.at[direction, slot],
-                relay_send.at[direction, slot], relay_recv.at[direction, slot],
+                from_core[part].at[place + direction], relay[part].at[direction, slot],
+                relay_send.at[part, direction, slot], relay_recv.at[part, direction, slot],
                 beside(direction),
             )
 
         def inbox_copy(direction, slot, place):
             return remote(
-                from_core.at[pl.ds(place, CHUNK)], inbox.at[direction, slot],
-                inbox_send.at[direction, slot], inbox_recv.at[direction, slot],
+                from_core[part].at[pl.ds(place, CHUNK)], inbox[part].at[direction, slot],
+                inbox_send.at[part, direction, slot], inbox_recv.at[part, direction, slot],
                 beside(direction),
             )
 
         def second_copy(ib, place):
             return remote(
-                from_core.at[pl.ds(place, CHUNK)], second_in.at[ib],
-                second_send.at[ib], second_recv.at[ib], across(order_in(ib)),
+                from_core[part].at[pl.ds(place, CHUNK)], second_in[part].at[ib],
+                second_send.at[part, ib], second_recv.at[part, ib], across(order_in(ib)),
             )
 
         def gram_units(first):
@@ -360,14 +364,17 @@
                 d = first + u
                 tops = []
                 for h in range(2):
-                    a, b = pair_places(assign, pairing, 0, d, h)
-                    tops.append(gram_top(source, a, b, h == 1))
-                    slots = slot_at(pairing[1, d], h)
+                    if part == 0:
+                        a, b = pair_places(assign, pairing, 0, d, h)
+                        tops.append(gram_top(source, a, b, h == 1))
+                        continue
                     around = [
-                        pair_around(assign, pairing, *home_of(pairing, d, slot)) for slot in slots
+                        pair_around(assign, pairing, *home_of(pairing, d, slot))
+                        for slot in slot_at(pairing[1, d], h)
                     ]
-                    packed[d, pl.ds(64 + 64 * h, 64)] = cross_top(source, *around)
-                packed[d, pl.ds(0, 64)] = pack(*tops)
+                    packed[part][d, pl.ds(64 * h, 64)] = cross_top(source, *around)
+                if part == 0:
+                    packed[part][d] = pack(*tops)
 
         def compute(step):
             da, db = order_in(step // 4), order_in(lax.rem(step, 4))
@@ -378,14 +385,14 @@
         def inbox_sum(slot):
             for direction in range(2):
                 inbox_copy(direction, slot, 0).wait_recv()
-            return inbox[0, slot] + inbox[1, slot]
+            return inbox[part][0, slot] + inbox[part][1, slot]
 
         def ship(step):
             ia, ib = step // 4, lax.rem(step, 4)
             place = my_chunk(order_in(ia), order_in(ib))
             chunk = pl.ds(place, CHUNK)
             core_copy(step).wait_recv()
-            from_core[chunk] += packed[pl.ds(core * half + place, CHUNK)]
+            from_core[part][chunk] += packed[part][pl.ds(core * half + place, CHUNK)]
 
             @pl.when(ia == 0)
             def _():
@@ -397,66 +404,63 @@
                 @pl.when(ia == 1 + direction)
                 def _(direction=direction):
                     relay_copy(direction, ib, place).wait_recv()
-                    from_core[place + direction] += relay[direction, ib]
+                    from_core[part][place + direction] += relay[part][direction, ib]
                     inbox_copy(direction, ib, place).start()
 
             @pl.when(ia == 3)
             def _():
-                from_core[chunk] += inbox_sum(ib)
+                from_core[part][chunk] += inbox_sum(ib)
                 second_copy(ib, place).start()
 
         def advance(step):
             compute(step)
             ship(step - 1)
 
-        compute(0)
-        each(1, 16, advance)
-        core_copy(15).wait_recv()
-        place = my_chunk(0, 0)
-        total[...] = (
-            from_core[pl.ds(place, CHUNK)]
-            + packed[pl.ds(core * half + place, CHUNK)]
-            + inbox_sum(3)
-        )
-        for ib in range(3):
-            second_copy(ib, 0).wait_recv()
-            total[...] += second_in[ib]
-
-        for part, size in enumerate(SLICES):
+        def close():
+            core_copy(15).wait_recv()
+            place = my_chunk(0, 0)
+            total[part][...] = (
+                from_core[part][pl.ds(place, CHUNK)]
+                + packed[part][pl.ds(core * half + place, CHUNK)]
+                + inbox_sum(3)
+            )
+            for ib in range(3):
+                second_copy(ib, 0).wait_recv()
+                total[part][...] += second_in[part][ib]
+            size = SLICES[part]
             for k in range(NZ):
-                begin = 64 * part + k * size
-                slices[part][k] = total[:, begin : begin + size, :]
-
-        def zr_copy(part, step):
+                slices[part][k] = total[part][:, k * size : (k + 1) * size, :]
+            for step in far_first:
+                zr_copy(step).start()
+
+        def zr_copy(step):
             return remote(
                 slices[part].at[lax.rem(z + step, NZ)], from_z[part].at[step],
                 zr_send.at[part, step], zr_recv.at[part, step], ring_device(step),
             )
 
-        def zg_copy(part, step):
+        def zg_copy(step):
             return remote(
                 mine_z[part], gathered[part].at[z], zg_send.at[part, step], zg_recv.at[part, step],
                 ring_device(step),
             )
 
         far_first = (4, 3, 5, 2, 6, 1, 7)
-        for part in range(2):
-            for step in far_first:
-                zr_copy(part, step).start()
-        for part in range(2):
+
+        def settle():
             acc = slices[part][z]
             for step in reversed(far_first):
-                zr_copy(part, step).wait_recv()
+                zr_copy(step).wait_recv()
                 acc = acc + from_z[part][step]
             mine_z[part][...] = acc
             for step in far_first:
-                zg_copy(part, step).start()
+                zg_copy(step).start()
             gathered[part][z] = acc
 
-        def units_of(part):
+        def units():
             for step in reversed(far_first):
-                zg_copy(part, step).wait_recv()
-            return [gathered[part][:, u].reshape(NZ * SLICES[part], 128) for u in range(CHUNK)]
+                zg_copy(step).wait_recv()
+            return [gathered[part][:, u].reshape(DEPTHS[part], 128) for u in range(CHUNK)]
 
         def drain_core(step):
             core_copy(step).wait_send()
@@ -470,9 +474,8 @@
             second_copy(ib, 0).wait_send()
 
         def drain_z(step):
-            for part in range(2):
-                zr_copy(part, step).wait_send()
-                zg_copy(part, step).wait_send()
+            zr_copy(step).wait_send()
+            zg_copy(step).wait_send()
 
         def drain():
             each(0, 16, drain_core)
@@ -480,7 +483,7 @@
             each(0, 3, drain_second)
             each(1, NZ, drain_z)
 
-        return units_of, drain
+        return compute, advance, close, settle, units, drain
 
     def handing(rnd, source):
         mine = core * half + my_chunk(0, 0)
@@ -569,7 +572,7 @@
             apply_units(other_units(step), 16 + step)
 
         def begin():
-            for ib in (3, 2, 1):
+            for ib in (1, 2, 3):
                 wsecond_copy(ib, mine).start()
             for direction in range(2):
                 wfull_copy(direction, 0, mine).start()
@@ -593,13 +596,22 @@
 
         return begin, forward, use, use_other, drain
 
-    units_of, drain_reduced = reduced()
+    compute_g, advance_g, close_g, settle_g, units_g, drain_g = reduction(0)
+    compute_c, advance_c, close_c, settle_c, units_c, drain_c = reduction(1)
+    compute_g(0)
+    each(1, 16, advance_g)
+    compute_c(0)
+    each(1, 9, advance_c)
+    close_g()
+    each(9, 16, advance_c)
+    settle_g()
+    close_c()
     begin0, forward0, use0, use_other0, drain0 = handing(0, (high0, low0))
     begin1, forward1, use1, use_other1, drain1 = handing(1, (high1, low1))
     mine = core * half + my_chunk(0, 0)
 
     tops = []
-    for unit in units_of(0):
+    for unit in units_g():
         tops.extend(unpack(unit))
     roots = inverse_roots(tops)
 
@@ -631,13 +643,14 @@
         use0(step)
         use_other0(step - 1)
 
+    settle_c()
     each(1, 4, take0)
-    crosses = units_of(1)
     for which in range(2):
         near_copy(which).wait_recv()
         for kind, table in enumerate((roots_near, grams_near)):
             for h, top in enumerate(unpack(near_in[which, kind])):
                 table[6 * which + h] = top
+    crosses = units_c()
 
     tops = []
     for u in range(CHUNK):
@@ -653,11 +666,18 @@
                 roots_near[left], crosses[u][64 * h : 64 * h + 64], roots_near[right]
             )
             tops.append(next_gram(cross, grams_near[left], grams_near[right], side_u, side_v))
+    each(4, 8, forward0)
     roots = inverse_roots(tops)
     for u in range(CHUNK):
         weights[1, mine + u] = packed_pair(roots, u)
     begin1()
-    each(4, 12, take0)
+
+    def late0(step):
+        use0(step)
+        use_other0(step - 1)
+
+    each(4, 8, late0)
+    each(8, 12, take0)
     each(1, 4, forward1)
     each(12, 16, take0)
     use_other0(15)
@@ -676,7 +696,8 @@
     each(4, 8, take1)
     each(8, 16, forward_and_take1)
     use_other1(15)
-    drain_reduced()
+    drain_g()
+    drain_c()
     drain0()
     drain1()
     for which in range(2):
@@ -727,16 +748,22 @@
             pltpu.VMEM((GROUPS, 64, 2 * STEP, 128), F32),
             pltpu.VMEM(TABLE, F32),
             part, part, part, part,
-            pltpu.VMEM((UNITS, DEPTH, 128), F32),
-            pltpu.VMEM((UNITS // 2, DEPTH, 128), F32),
-            pltpu.VMEM((2, 4, DEPTH, 128), F32),
-            pltpu.VMEM((2, 4, CHUNK, DEPTH, 128), F32),
-            pltpu.VMEM((3, CHUNK, DEPTH, 128), F32),
-            pltpu.VMEM((CHUNK, DEPTH, 128), F32),
+            pltpu.VMEM((UNITS, DEPTHS[0], 128), F32),
+            pltpu.VMEM((UNITS // 2, DEPTHS[0], 128), F32),
+            pltpu.VMEM((2, 4, DEPTHS[0], 128), F32),
+            pltpu.VMEM((2, 4, CHUNK, DEPTHS[0], 128), F32),
+            pltpu.VMEM((3, CHUNK, DEPTHS[0], 128), F32),
+            pltpu.VMEM((CHUNK, DEPTHS[0], 128), F32),
             pltpu.VMEM((NZ, CHUNK, SLICES[0], 128), F32),
             pltpu.VMEM((NZ, CHUNK, SLICES[0], 128), F32),
             pltpu.VMEM((CHUNK, SLICES[0], 128), F32),
             pltpu.VMEM((NZ, CHUNK, SLICES[0], 128), F32),
+            pltpu.VMEM((UNITS, DEPTHS[1], 128), F32),
+            pltpu.VMEM((UNITS // 2, DEPTHS[1], 128), F32),
+            pltpu.VMEM((2, 4, DEPTHS[1], 128), F32),
+            pltpu.VMEM((2, 4, CHUNK, DEPTHS[1], 128), F32),
+            pltpu.VMEM((3, CHUNK, DEPTHS[1], 128), F32),
+            pltpu.VMEM((CHUNK, DEPTHS[1], 128), F32),
             pltpu.VMEM((NZ, CHUNK, SLICES[1], 128), F32),
             pltpu.VMEM((NZ, CHUNK, SLICES[1], 128), F32),
             pltpu.VMEM((CHUNK, SLICES[1], 128), F32),
@@ -747,8 +774,7 @@
             pltpu.VMEM((8, 64, 128), F32),
             pltpu.VMEM((2, 2, 64, 128), F32),
             dma((GROUPS,)), dma((32,)),
-            dma((16,)), dma((16,)), dma((2, 4)), dma((2, 4)), dma((2, 4)), dma((2, 4)),
-            dma((4,)), dma((4,)), ring, ring, ring, ring,
+            chunks, chunks, plane, plane, plane, plane, second, second, ring, ring, ring, ring,
             plane, plane, plane, plane, second, second, chunks, chunks, dma((2,)), dma((2,)),
         ],
         compiler_params=PARAMS(collective_id=0, has_side_effects=True),

time: 97.7 us -> 100 us (1.024)
  Pallas kernels: 97.6 us -> 100 us
    pallas_call x1, Pallas kernels: 89.9 us -> 92.6 us  [rounds(): pl.pallas_call(fused_kernel, out_shape=jax.ShapeDtypeStruct(TABLE, F32),...]
where the time goes in v7:
time: 100 us
  Pallas kernels  100 us (100%)
    pallas_call x1, Pallas kernels, rounds(): pl.pallas_call(fused_kernel, out_shape=jax.ShapeDtypeStruct(TABLE, F32),...  92.6 us
    pallas_call x1, Pallas kernels, unturned(): pl.pallas_call(last_kernel, out_shape=jax.ShapeDtypeStruct(shape, F32), g...  7.72 us

profile of v7, /device:TPU:1, one launch (start us, length us, event | category | flops | bytes accessed | tf_op | source)
XLA Modules:
  0.0 100.3 jit_solution(4116189714251663809)
XLA Ops:
  0.0 92.6 %rounds.1.source = f32[256,32,128]{2,1,0:T(8,128)} custom-call(s32[256]{0:T(256)} %assign.3, s32[2,64]{1,0:T(2,128)} %pairing.3, f32[64,128,128]{2,1,0:T(8,128)} %bitcast.10), custom_call_target="tpu_custom_call" | custom-call | tf_op jit(solution)/shard_map/rounds/pallas_call | solution.py:742
  92.6 7.7 %unturn.1 = f32[64,128,128]{2,1,0:T(8,128)} custom-call(s32[256]{0:T(256)} %assign.3, s32[2,64]{1,0:T(2,128)} %pairing.3, f32[256,32,128]{2,1,0:T(8,128)} %rounds.1.source), custom_call_target="tpu_custom_call" | custom-call | tf_op jit(solution)/shard_map/unturn/pallas_call | solution.py:787

commit v8 on v7

--- a/solution.py
+++ b/solution.py
@@ -412,9 +412,11 @@
                 from_core[part][chunk] += inbox_sum(ib)
                 second_copy(ib, place).start()
 
+        lag = 3 - part
+
         def advance(step):
             compute(step)
-            ship(step - 1)
+            ship(step - lag)
 
         def close():
             core_copy(15).wait_recv()
@@ -483,7 +485,7 @@
             each(0, 3, drain_second)
             each(1, NZ, drain_z)
 
-        return compute, advance, close, settle, units, drain
+        return compute, advance, ship, close, settle, units, drain
 
     def handing(rnd, source):
         mine = core * half + my_chunk(0, 0)
@@ -596,14 +598,17 @@
 
         return begin, forward, use, use_other, drain
 
-    compute_g, advance_g, close_g, settle_g, units_g, drain_g = reduction(0)
-    compute_c, advance_c, close_c, settle_c, units_c, drain_c = reduction(1)
-    compute_g(0)
-    each(1, 16, advance_g)
-    compute_c(0)
-    each(1, 9, advance_c)
+    compute_g, advance_g, ship_g, close_g, settle_g, units_g, drain_g = reduction(0)
+    compute_c, advance_c, ship_c, close_c, settle_c, units_c, drain_c = reduction(1)
+    each(0, 3, compute_g)
+    each(3, 16, advance_g)
+    for step in range(2):
+        compute_c(step)
+        ship_g(13 + step)
+    each(2, 10, advance_c)
     close_g()
-    each(9, 16, advance_c)
+    each(10, 16, advance_c)
+    ship_c(14)
     settle_g()
     close_c()
     begin0, forward0, use0, use_other0, drain0 = handing(0, (high0, low0))
@@ -641,7 +646,6 @@
     def take0(step):
         forward0(step)
         use0(step)
-        use_other0(step - 1)
 
     settle_c()
     each(1, 4, take0)
@@ -674,28 +678,25 @@
 
     def late0(step):
         use0(step)
-        use_other0(step - 1)
-
-    each(4, 8, late0)
-    each(8, 12, take0)
+        use_other0(step - 4)
+
+    def late1(step):
+        use1(step)
+        use_other1(step - 4)
+
+    each(8, 16, forward0)
+    each(4, 12, late0)
     each(1, 4, forward1)
-    each(12, 16, take0)
-    use_other0(15)
-    use1(0)
-
-    def take1(step):
-        use1(step)
-        use_other1(step - 1)
-
-    def forward_and_take1(step):
-        forward1(step)
-        take1(step)
-
-    each(1, 4, take1)
-    each(4, 8, forward1)
-    each(4, 8, take1)
-    each(8, 16, forward_and_take1)
-    use_other1(15)
+    each(12, 16, late0)
+    each(12, 16, use_other0)
+    each(0, 4, use1)
+    each(0, 4, use_other1)
+    each(4, 12, forward1)
+    each(4, 8, use1)
+    each(8, 12, late1)
+    each(12, 16, forward1)
+    each(12, 16, late1)
+    each(12, 16, use_other1)
     drain_g()
     drain_c()
     drain0()

time: 100 us -> 104 us (1.040); the launches traced: 100 us -> 103 us
  Pallas kernels: 100 us -> 103 us
    pallas_call x1, Pallas kernels: 92.6 us -> 95.1 us  [rounds(): pl.pallas_call(fused_kernel, out_shape=jax.ShapeDtypeStruct(TABLE, F32),...]
where the time goes in v8:
time: 104 us; the launch traced here: 103 us
  Pallas kernels  103 us (99%)
    pallas_call x1, Pallas kernels, rounds(): pl.pallas_call(fused_kernel, out_shape=jax.ShapeDtypeStruct(TABLE, F32),...  95.1 us
    pallas_call x1, Pallas kernels, unturned(): pl.pallas_call(last_kernel, out_shape=jax.ShapeDtypeStruct(shape, F32), g...  7.72 us

profile of v8, /device:TPU:1, one launch (start us, length us, event | category | flops | bytes accessed | tf_op | source)
XLA Modules:
  0.0 102.8 jit_solution(7285693750044321230)
XLA Ops:
  0.0 95.1 %rounds.1.source = f32[256,32,128]{2,1,0:T(8,128)} custom-call(s32[256]{0:T(256)} %assign.3, s32[2,64]{1,0:T(2,128)} %pairing.3, f32[64,128,128]{2,1,0:T(8,128)} %bitcast.10), custom_call_target="tpu_custom_call" | custom-call | tf_op jit(solution)/shard_map/rounds/pallas_call | solution.py:743
  95.1 7.7 %unturn.1 = f32[64,128,128]{2,1,0:T(8,128)} custom-call(s32[256]{0:T(256)} %assign.3, s32[2,64]{1,0:T(2,128)} %pairing.3, f32[256,32,128]{2,1,0:T(8,128)} %rounds.1.source), custom_call_target="tpu_custom_call" | custom-call | tf_op jit(solution)/shard_map/unturn/pallas_call | solution.py:788

commit v9 on v6

--- a/solution.py
+++ b/solution.py
@@ -569,7 +569,7 @@
             apply_units(other_units(step), 16 + step)
 
         def begin():
-            for ib in (3, 2, 1):
+            for ib in (1, 2, 3):
                 wsecond_copy(ib, mine).start()
             for direction in range(2):
                 wfull_copy(direction, 0, mine).start()
@@ -683,9 +683,12 @@
         near_copy(which).wait_send()
 
 
-def last_kernel(assign, pairing, source, out, places):
+def last_kernel(assign, pairing, blocks, out, places, source, sem):
     @pl.when(pl.program_id(0) == 0)
     def _():
+        copy = pltpu.make_async_copy(blocks, source, sem)
+        copy.start()
+
         def unit(d, carry):
             up = jnp.where(d == UNITS - 1, 0, d + 1)
             down = jnp.where(d == 0, UNITS - 1, d - 1)
@@ -699,6 +702,7 @@
             return carry
 
         lax.fori_loop(0, UNITS, unit, 0, unroll=4)
+        copy.wait()
 
     flat = out.reshape(64 * 2 * STEP, 128)
     for k in range(STEP):
@@ -762,9 +766,11 @@
         last_kernel,
         out_shape=jax.ShapeDtypeStruct(shape, F32),
         grid=(BLOCKS // 4 // STEP,),
-        in_specs=[SMEM, SMEM, VMEM],
+        in_specs=[SMEM, SMEM, pl.BlockSpec(memory_space=pl.ANY)],
         out_specs=pl.BlockSpec((64, 2 * STEP, 128), lambda i: (0, i, 0)),
-        scratch_shapes=[pltpu.SMEM((BLOCKS,), jnp.int32)],
+        scratch_shapes=[
+            pltpu.SMEM((BLOCKS,), jnp.int32), pltpu.VMEM(TABLE, F32), pltpu.SemaphoreType.DMA
+        ],
         compiler_params=PARAMS(),
         name="unturn",
     )(assignment, pairing, source)

time: 97.7 us -> 98.2 us (level)
  no operation moved by 1% of the time
where the time goes in v9:
time: 98.2 us; the launch traced here: 98.1 us
  Pallas kernels  98.1 us (100%)
    pallas_call x1, Pallas kernels, rounds(): pl.pallas_call(fused_kernel, out_shape=jax.ShapeDtypeStruct(TABLE, F32),...  90.7 us
    pallas_call x1, Pallas kernels, unturned(): pl.pallas_call(last_kernel, out_shape=jax.ShapeDtypeStruct(shape, F32), g...  7.39 us

profile of v9, /device:TPU:1, one launch (start us, length us, event | category | flops | bytes accessed | tf_op | source)
XLA Modules:
  0.0 98.1 jit_solution(12304848794383650203)
XLA Ops:
  0.0 90.7 %rounds.1.blocks = f32[256,32,128]{2,1,0:T(8,128)} custom-call(s32[256]{0:T(256)} %assign.3, s32[2,64]{1,0:T(2,128)} %pairing.3, f32[64,128,128]{2,1,0:T(8,128)} %bitcast.10), custom_call_target="tpu_custom_call" | custom-call | tf_op jit(solution)/shard_map/rounds/pallas_call | solution.py:725
  90.7 7.4 %unturn.1 = f32[64,128,128]{2,1,0:T(8,128)} custom-call(s32[256]{0:T(256)} %assign.3, s32[2,64]{1,0:T(2,128)} %pairing.3, f32[256,32,128]{2,1,0:T(8,128)} %rounds.1.blocks), custom_call_target="tpu_custom_call" | custom-call | tf_op jit(solution)/shard_map/unturn/pallas_call | solution.py:765

commit v10 on v9

--- a/solution.py
+++ b/solution.py
@@ -701,7 +701,7 @@
             places[assign[SLOTS * d + 3]] = SLOTS * d + jnp.where(here == 2, 1, 3)
             return carry
 
-        lax.fori_loop(0, UNITS, unit, 0, unroll=4)
+        lax.fori_loop(0, UNITS, unit, 0, unroll=16)
         copy.wait()
 
     flat = out.reshape(64 * 2 * STEP, 128)

time: 98.2 us -> 98.2 us (level)
  no operation moved by 1% of the time
where the time goes in v10:
time: 98.2 us; the launch traced here: 98.1 us
  Pallas kernels  98.1 us (100%)
    pallas_call x1, Pallas kernels, rounds(): pl.pallas_call(fused_kernel, out_shape=jax.ShapeDtypeStruct(TABLE, F32),...  90.7 us
    pallas_call x1, Pallas kernels, unturned(): pl.pallas_call(last_kernel, out_shape=jax.ShapeDtypeStruct(shape, F32), g...  7.39 us

profile of v10, /device:TPU:1, one launch (start us, length us, event | category | flops | bytes accessed | tf_op | source)
XLA Modules:
  0.0 98.1 jit_solution(5627458451723115669)
XLA Ops:
  0.0 90.7 %rounds.1.blocks = f32[256,32,128]{2,1,0:T(8,128)} custom-call(s32[256]{0:T(256)} %assign.3, s32[2,64]{1,0:T(2,128)} %pairing.3, f32[64,128,128]{2,1,0:T(8,128)} %bitcast.10), custom_call_target="tpu_custom_call" | custom-call | tf_op jit(solution)/shard_map/rounds/pallas_call | solution.py:725
  90.7 7.4 %unturn.1 = f32[64,128,128]{2,1,0:T(8,128)} custom-call(s32[256]{0:T(256)} %assign.3, s32[2,64]{1,0:T(2,128)} %pairing.3, f32[256,32,128]{2,1,0:T(8,128)} %rounds.1.blocks), custom_call_target="tpu_custom_call" | custom-call | tf_op jit(solution)/shard_map/unturn/pallas_call | solution.py:765
